TPU v7x, 32 devices: a whole 2x2x4 slice. The times are simulated.
32 devices in a mesh: fsdp: 8 (over z, y), grp: 4 (over x, core).
Axes of the slice: x: 2, y: 2, z: 4, core: 2. Of those that a mesh axis runs over, the one named last changes fastest.
Arguments:
- weight: bfloat16 [26624, 8192], P('fsdp', 'grp'), may hold values from -6 to 6
Outputs:
- quantized: bfloat16 [26624, 8192], P('grp', 'fsdp')
- scales: float32 [208, 64], P('grp', 'fsdp')
All inputs are finite; a program needn't handle non-finite values. Where the computation divides by a largest or mean magnitude, that divisor is 1e-20 or more.
Results may differ from a plain program's by a relative error of at most 0.001.
Values sent between devices are 32-bit elements; how exact they have to be, the bound alone decides.
No kernel may reach another device: no remote copies, remote signals or barrier semaphores. Data moves between devices by JAX's collectives and lax.ppermute only.
A program may use at most 192 MiB of HBM per device.

v0:
```python
import math

import jax
import jax.numpy as jnp
import numpy as np
from jax import lax
from jax.sharding import PartitionSpec as P

D = 8192
BLOCK = 128
FF = 26624


def paley_signs():
    squares_set = set()
    for coord_one in range(5):
        for coord_two in range(5):
            if coord_one or coord_two:
                squares_set.add(
                    (
                        (coord_one * coord_one + 2 * coord_two * coord_two) % 5,
                        2 * coord_one * coord_two % 5,
                    )
                )
    conference = np.zeros((26, 26), np.float32)
    conference[0, 1:] = 1.0
    conference[1:, 0] = 1.0
    for row_elem in range(25):
        for col_elem in range(25):
            diff_one = (row_elem % 5 - col_elem % 5) % 5
            diff_two = (row_elem // 5 - col_elem // 5) % 5
            if diff_one or diff_two:
                conference[1 + row_elem, 1 + col_elem] = (
                    1.0 if (diff_one, diff_two) in squares_set else -1.0
                )
    plus_block = np.array([[1.0, 1.0], [1.0, -1.0]], np.float32)
    minus_block = np.array([[1.0, -1.0], [-1.0, -1.0]], np.float32)
    return (
        np.kron(conference, plus_block) + np.kron(np.eye(26, dtype=np.float32), minus_block)
    ).astype(np.float32)


def sign_table(order, dtype):
    if order <= 64:
        indices = lax.iota(jnp.int32, order)
        parity = jnp.zeros((order, order), jnp.int32)
        for bit_pos in range(max(order.bit_length() - 1, 0)):
            parity = parity + (indices[:, None] >> bit_pos & 1) * (indices[None, :] >> bit_pos & 1)
        return (1 - 2 * (parity & 1)).astype(dtype)
    outer_part = sign_table(order // 64, dtype)
    inner_part = sign_table(64, dtype)
    return (outer_part[:, None, :, None] * inner_part[None, :, None, :]).reshape(order, order)


def body(weight):
    exact_prec = lax.Precision.HIGHEST
    rows_dev, cols_dev = weight.shape
    parts = lax.axis_size("fsdp")
    groups = lax.axis_size("grp")
    sub_rows = rows_dev // 52
    piece = cols_dev // parts
    piece_signs = sign_table(piece, jnp.bfloat16)
    parts_signs = sign_table(parts, jnp.float32)
    paley = jnp.asarray(paley_signs(), jnp.float32)
    sub_signs = sign_table(sub_rows, jnp.float32)
    group_signs = sign_table(groups, jnp.float32)
    inner_done = jnp.einsum(
        "rab,bj->raj",
        weight.reshape(rows_dev, parts, piece),
        piece_signs,
        preferred_element_type=jnp.float32,
    )
    rotated = jnp.einsum("ap,raj->prj", parts_signs, inner_done, precision=exact_prec)
    rotated = rotated.reshape(parts, sub_rows, 52, piece)
    rotated = jnp.einsum("ab,pcbj->pcaj", paley, rotated, precision=exact_prec)
    rotated = jnp.einsum("ce,peaj->pcaj", sub_signs, rotated, precision=exact_prec)
    rotated = rotated.reshape(parts, sub_rows, 52 * piece)
    fsdp_signs = sign_table(parts, jnp.float32)
    mixed = jnp.einsum(
        "fg,gnx->fnx",
        fsdp_signs,
        lax.all_to_all(rotated, "fsdp", split_axis=0, concat_axis=0, tiled=True),
        precision=exact_prec,
    )
    count = mixed.shape[1]
    stacked = mixed.reshape(1, parts, count, 52 * piece)
    moved = lax.all_to_all(stacked, "grp", split_axis=1, concat_axis=0, tiled=True)
    moved = moved.reshape(groups, parts // groups, count, 52, piece)
    result = jnp.einsum("qg,gmnaj->mnaqj", group_signs, moved, precision=exact_prec)
    cols_out = groups * piece
    final = result.reshape(-1, cols_out) * (1.0 / math.sqrt(FF * D))
    rows_out = final.shape[0]
    blocks = final.reshape(rows_out // BLOCK, BLOCK, cols_out // BLOCK, BLOCK)
    scales = jnp.max(jnp.abs(blocks), axis=(1, 3))
    quantized = (
        (blocks / (scales[:, None, :, None] + 1e-06))
        .astype(jnp.bfloat16)
        .reshape(rows_out, cols_out)
    )
    return (quantized, scales)


def solution(mesh):
    in_specs = (P("fsdp", "grp"),)
    out_specs = (P("grp", "fsdp"), P("grp", "fsdp"))
    return jax.shard_map(body, mesh=mesh, in_specs=in_specs, out_specs=out_specs, check_vma=False)
```

profile of v0, /device:TPU:1, one launch (start us, length us, event | category | flops | bytes accessed | tf_op | source)
XLA Modules:
  0.0 1330.5 jit_solution(17154876967371506080)
XLA Ops:
  0.7 0.1 fusion.62
  0.8 0.4 copy-done.1
  1.2 0.1 fusion.25
  1.3 0.2 broadcast_multiply_fusion
  1.5 0.2 reshape.432
  1.7 14.2 %copy.27 = bf16[416,8,8,256]{3,2,1,0:T(8,128)(2,1)} copy(bf16[416,8,8,256]{3,1,2,0:T(8,128)(2,1)} %bitcast.62) | data formatting | bytes 27262976
  15.9 13.8 %fusion.77 = f32[256,3328,8]{0,2,1:T(8,128)} fusion(bf16[256,256,1]{1,0,2:T(8,128)(2,1)S(1)} %reshape.432, bf16[3328,8,256]{2,1,0:T(8,128)(2,1)} %bitcast.63), kind=kOutput, calls=%fused_computation.87 | convolution fusion | flops 3489660928 | bytes 41025536 | tf_op jit(solution)/shard_map/rab,bj->raj/dot_general | solution.py:67
  29.7 28.4 %fusion.3 = f32[8,3328,256]{2,0,1:T(8,128)} fusion(f32[256,3328,8]{0,2,1:T(8,128)} %fusion.77, s32[8]{0:T(128)S(1)} %get-tuple-element.12, s32[8]{0:T(128)S(1)} %get-tuple-element.13, s32[8]{0:T(128)S(1)} %shift-right-arithmetic_and_fusion.10), kind=kOutput, calls=%fused_computation.4 | convolution fusion | flops 654312000 | bytes 54526048 | tf_op jit(solution)/shard_map/ap,raj->prj/dot_general | solution.py:73
  58.1 41.6 %fusion.17 = f32[8,64,52,256]{3,2,1,0:T(8,128)} fusion(f32[52,52,1,1]{1,0,3,2:T(8,128)S(1)} %copy-done, f32[8,64,52,256]{3,0,2,1:T(8,128)} %bitcast.58), kind=kOutput, calls=%fused_computation.15 | convolution fusion | flops 4253024256 | bytes 54536768 | tf_op jit(solution)/shard_map/ab,pcbj->pcaj/dot_general | solution.py:75
  99.8 37.8 %fusion.20 = f32[8,52,8,8,256]{4,3,2,1,0:T(8,128)} fusion(f32[8,64,52,256]{3,2,1,0:T(8,128)} %fusion.17, s32[64]{0:T(128)S(1)} %get-tuple-element.4, s32[64]{0:T(128)S(1)} %get-tuple-element.5, s32[64]{0:T(128)S(1)} %get-tuple-element.6, s32[64]{0:T(128)S(1)} %get-tuple-element.7, s32[64]{0:T(128)S(1)} %get-tuple-element.8, s32[64]{0:T(128)S(1)} %get-tuple-element.9), kind=kOutput, calls=%fused_computation.16 | convolution fusion | flops 5234552832 | bytes 54527488 | tf_op jit(solution)/shard_map/ce,peaj->pcaj/dot_general | solution.py:76
  137.6 11.2 copy.26
  148.8 593.4 %all_to_all.14 = f32[8,64,13312]{2,1,0:T(8,128)} all-to-all(f32[8,64,13312]{2,1,0:T(8,128)S(1)} %bitcast.61), channel_id=1, replica_groups=mesh['fsdp'=8,'grp'=4] {'fsdp'}, dimensions={0} | all-to-all | bytes 54525952 | tf_op jit(solution)/shard_map/all_to_all | solution.py:82
  742.2 47.3 %fusion.11 = f32[1,8,64,13312]{3,1,2,0:T(8,128)} fusion(f32[8,64,13312]{2,1,0:T(8,128)} %all_to_all.14, s32[8]{0:T(128)S(1)} %get-tuple-element.12, s32[8]{0:T(128)S(1)} %get-tuple-element.13, s32[8]{0:T(128)S(1)} %shift-right-arithmetic_and_fusion.10), kind=kOutput, calls=%fused_computation.13 | convolution fusion | flops 654312000 | bytes 54526048 | tf_op jit(solution)/shard_map/fg,gnx->fnx/dot_general | solution.py:79
  789.5 14.4 %copy.18 = f32[1,8,64,13312]{3,2,0,1:T(8,128)S(1)} copy(f32[1,8,64,13312]{3,1,2,0:T(8,128)} %fusion.11) | data formatting | bytes 54525952 | tf_op jit(solution)/shard_map/reshape | solution.py:86
  803.9 301.3 %all_to_all.15 = f32[1,8,64,13312]{3,2,0,1:T(8,128)} all-to-all(f32[1,8,64,13312]{3,2,0,1:T(8,128)S(1)} %copy.18), channel_id=1, replica_groups=mesh['fsdp'=8,'grp'=4] {'grp'}, dimensions={1} | all-to-all | bytes 54525952 | tf_op jit(solution)/shard_map/all_to_all | solution.py:87
  1105.2 27.9 %reshape.431 = f32[4,2,64,52,256]{4,3,2,1,0:T(8,128)} reshape(f32[1,8,64,13312]{3,2,0,1:T(8,128)} %all_to_all.15) | data formatting | bytes 54525952 | tf_op jit(solution)/shard_map/reshape | solution.py:88
  1133.1 75.1 %fusion.14 = f32[2,64,52,256,4]{3,4,2,1,0:T(4,128)} fusion(f32[4,2,64,52,256]{4,3,2,1,0:T(8,128)} %reshape.431, s32[4]{0:T(128)S(1)} %copy-done.2, s32[4]{0:T(128)S(1)} %copy-done.4), kind=kOutput, calls=%fused_computation.14 | convolution fusion | flops 333971584 | bytes 54525984 | tf_op jit(solution)/shard_map/qg,gmnaj->mnaqj/dot_general | solution.py:89
  1208.2 18.8 %abs_bitcast_fusion = f32[2,64,52,4,256]{4,3,2,1,0:T(4,128)} fusion(f32[2,64,52,256,4]{3,4,2,1,0:T(4,128)} %fusion.14), kind=kLoop, calls=%fused_computation.12 | loop fusion | flops 6815744 | bytes 54525952 | tf_op jit(solution)/shard_map/abs | solution.py:94
  1227.0 31.9 %abs.11 = f32[52,128,8,128]{3,2,1,0:T(8,128)} reshape(f32[2,64,52,4,256]{4,3,2,1,0:T(4,128)} %abs_bitcast_fusion) | data formatting | bytes 54525952 | tf_op jit(solution)/shard_map/abs | solution.py:94
  1259.0 9.7 reduce_max.9
  1268.6 0.7 copy.20
  1269.3 25.0 %copy.28 = f32[832,8,4,256]{3,1,2,0:T(8,128)} copy(f32[832,8,4,256]{3,2,1,0:T(4,128)} %bitcast.57) | data formatting | bytes 54525952
  1294.3 10.8 div.11
  1305.1 25.2 %fusion.2 = bf16[6656,1024]{1,0:T(8,128)(2,1)} fusion(f32[6656,1024]{1,0:T(8,128)} %bitcast.59, f32[832,8,8,128]{3,2,1,0:T(8,128)} %bitcast.60), kind=kLoop, calls=%fused_computation.3 | loop fusion | flops 13631488 | bytes 68157440 | tf_op jit(solution)/shard_map/convert_element_type | solution.py:97
  (16 shorter events, 0.1 us)
Async XLA Ops:
  0.7 0.5 copy-start.1
  0.7 0.5 copy-start.3
  29.7 28.4 %copy-start = (f32[52,52,1,1]{1,0,3,2:T(8,128)S(1)}, f32[52,52,1,1]{1,0,3,2:T(8,128)}, u32[]{:S(2)}) copy-start(f32[52,52,1,1]{1,0,3,2:T(8,128)} %constant.1) | copy-start | bytes 32452
  1105.2 27.9 %copy-start.2 = (s32[4]{0:T(128)S(1)}, s32[4]{0:T(128)}, u32[]{:S(2)}) copy-start(s32[4]{0:T(128)} %copy-done.1) | copy-start | bytes 52
  1105.2 27.9 %copy-start.4 = (s32[4]{0:T(128)S(1)}, s32[4]{0:T(128)}, u32[]{:S(2)}) copy-start(s32[4]{0:T(128)} %copy-done.3) | copy-start | bytes 52
where the time goes:
time: 1340 us; the launch traced here: 1330 us
  blocking collectives  895 us (67%)
  matrix products  244 us (18%)
  local copies, waits for them, and re-layouts  137 us (10%)
  other arithmetic  54.1 us (4%)
    all_to_all x1, blocking collectives, body(): lax.all_to_all(rotated, 'fsdp', split_axis=0, concat_axis=0, tiled=True)  593 us
    all_to_all x1, blocking collectives, body(): lax.all_to_all(stacked, 'grp', split_axis=1, concat_axis=0, tiled=True)  301 us
    dot_general x1, matrix products, body(): jnp.einsum('qg,gmnaj->mnaqj', group_signs, moved, precision=exact_prec)  75.1 us
    dot_general x1, matrix products, body(): jnp.einsum('fg,gnx->fnx', fsdp_signs, lax.all_to_all(rotated, 'fsdp', spl...  47.3 us
    dot_general x1, matrix products, body(): rotated = jnp.einsum('ab,pcbj->pcaj', paley, rotated, precision=exact_prec)  41.6 us
    unnamed x13, local copies, waits for them, and re-layouts  40.2 us
    dot_general x1, matrix products, body(): jnp.einsum('ce,peaj->pcaj', sub_signs, rotated, precision=exact_prec)  37.8 us
    abs x1, local copies, waits for them, and re-layouts, body(): scales = jnp.max(jnp.abs(blocks), axis=(1, 3))  31.9 us

commit v1 on v0

--- a/solution.py
+++ b/solution.py
@@ -1,14 +1,21 @@
+import functools
 import math
 
 import jax
 import jax.numpy as jnp
 import numpy as np
 from jax import lax
+from jax.experimental import pallas as pl
+from jax.experimental.pallas import tpu as pltpu
 from jax.sharding import PartitionSpec as P
 
 D = 8192
 BLOCK = 128
 FF = 26624
+PALEY = 52
+LANES = 128
+SPLIT = 2
+CHAINED = True
 
 
 def paley_signs():
@@ -40,6 +47,13 @@
     ).astype(np.float32)
 
 
+def sylvester(order):
+    table = np.ones((1, 1), np.float32)
+    while table.shape[0] < order:
+        table = np.kron(np.array([[1.0, 1.0], [1.0, -1.0]], np.float32), table)
+    return table
+
+
 def sign_table(order, dtype):
     if order <= 64:
         indices = lax.iota(jnp.int32, order)
@@ -52,7 +66,7 @@
     return (outer_part[:, None, :, None] * inner_part[None, :, None, :]).reshape(order, order)
 
 
-def body(weight):
+def plain_body(weight):
     exact_prec = lax.Precision.HIGHEST
     rows_dev, cols_dev = weight.shape
     parts = lax.axis_size("fsdp")
@@ -100,6 +114,455 @@
     return (quantized, scales)
 
 
+def parity_sign(bits, order):
+    parity = bits
+    shift = 1
+    while shift < order.bit_length():
+        parity = parity ^ (parity >> shift)
+        shift *= 2
+    return 1.0 - 2.0 * (parity & 1).astype(jnp.float32)
+
+
+def butterfly(values):
+    values = list(values)
+    half = 1
+    while half < len(values):
+        for low in range(len(values)):
+            if not low & half:
+                one, two = values[low], values[low + half]
+                values[low], values[low + half] = one + two, one - two
+        half *= 2
+    return values
+
+
+def compiler_params(limit):
+    return pltpu.CompilerParams(vmem_limit_bytes=limit)
+
+
+TINY = pl.CostEstimate(flops=0, bytes_accessed=0, transcendentals=0)
+ANYWHERE = pl.BlockSpec(memory_space=pl.ANY)
+
+
+class Labels:
+    def __init__(self, parts, groups):
+        self.parts_bits = parts.bit_length() - 1
+        self.groups_bits = groups.bit_length() - 1
+        self.slab_bits = self.parts_bits - self.groups_bits
+
+    def start(self):
+        return [("p", i) for i in range(self.parts_bits)]
+
+    def split(self, axis, bit):
+        return ("p" if axis == "fsdp" else "g", bit)
+
+    def made(self, axis, bit):
+        if axis == "grp":
+            return ("k", bit)
+        return ("m", bit) if bit < self.slab_bits else ("g", bit - self.slab_bits)
+
+
+def slot_of(labels, values):
+    return sum(values[label] << at for at, label in enumerate(labels))
+
+
+def values_of(labels, slot):
+    return {label: slot >> at & 1 for at, label in enumerate(labels)}
+
+
+class Stage:
+    def __init__(self, kind, bits):
+        self.kind, self.bits = kind, bits
+        self.fan = 1 << len(bits)
+
+    def send(self, arrays):
+        if self.kind == "all":
+            return [lax.all_to_all(arrays[0], self.bits[0][0], split_axis=0, concat_axis=0, tiled=True)]
+        if self.kind == "sum":
+            axis, bit = self.bits[0]
+            pairs = [[i, i ^ 1 << bit] for i in range(lax.axis_size(axis)) if not i >> bit & 1]
+            both = lax.psum_scatter(
+                arrays[0], axis, scatter_dimension=0, axis_index_groups=pairs, tiled=False
+            )
+            return [arrays[0], both]
+        received = [arrays[0]]
+        axes = {axis for axis, _ in self.bits}
+        sizes = {axis: lax.axis_size(axis) for axis in axes}
+        for e in range(1, self.fan):
+            masks = {axis: 0 for axis in axes}
+            for at, (axis, bit) in enumerate(self.bits):
+                masks[axis] |= (e >> at & 1) << bit
+            used = [axis for axis in ("fsdp", "grp") if masks.get(axis)]
+            assert len(used) == 1
+            axis = used[0]
+            pairs = [(i, i ^ masks[axis]) for i in range(sizes[axis])]
+            received.append(lax.ppermute(arrays[e], axis, pairs))
+        return received
+
+    def place(self):
+        if self.kind == "all":
+            return None
+        place = 0
+        for at, (axis, bit) in enumerate(self.bits):
+            place = place | ((lax.axis_index(axis) >> bit) & 1) << at
+        return place
+
+    def arrived(self, refs, *index):
+        if self.kind == "sum":
+            axis, bit = self.bits[0]
+            return [refs[0].at[(lax.axis_index(axis) >> bit & 1,) + index], refs[1].at[index]]
+        return self.views(refs, self.fan, *index)
+
+    def values(self, found):
+        return [found[0], found[1] - found[0]] if self.kind == "sum" else found
+
+    def views(self, refs, fan, *index):
+        if self.kind != "xor":
+            return [refs[0].at[(e,) + index] for e in range(fan)]
+        return [refs[e].at[index] for e in range(fan)]
+
+    def shapes(self, slots, rows, piece):
+        if self.kind != "xor":
+            return [jax.ShapeDtypeStruct((self.fan, slots, rows, piece), jnp.float32)]
+        return [jax.ShapeDtypeStruct((slots, rows, piece), jnp.float32)] * self.fan
+
+    def blocks(self, slots, rows, piece, moving, arrived=False):
+        where = (lambda step: (0, step, 0)) if moving else (lambda step: (0, 0, 0))
+        if self.kind != "xor":
+            whole = pl.BlockSpec((self.fan, slots, rows, piece), lambda step: (0,) + where(step))
+            after = [pl.BlockSpec((slots, rows, piece), where)] if self.kind == "sum" and arrived else []
+            return [whole] + after
+        return [pl.BlockSpec((slots, rows, piece), where)] * self.fan
+
+
+def combine(stage, made, values, absolute=False):
+    place, toward = stage.place(), None
+    for at, label in enumerate(made):
+        if label[0] == "g" and not absolute:
+            bit = ((lax.axis_index("grp") >> label[1]) & 1) << at
+            toward = bit if toward is None else toward | bit
+    if toward is not None:
+        values = [values[0]] + [
+            parity_sign(toward & e, stage.fan) * values[e] for e in range(1, stage.fan)
+        ]
+    sums = butterfly(values)
+    if place is not None:
+        toward = 0 if toward is None else toward
+        sums = [parity_sign((w ^ toward) & place, stage.fan) * sums[w] for w in range(stage.fan)]
+    return sums
+
+
+def make_pieces(weight, first, count, parts, after, stage, labels):
+    rows_dev, cols_dev = weight.shape
+    piece = cols_dev // parts
+    sub_rows = rows_dev // PALEY
+    rows = count * PALEY
+    order = sylvester(sub_rows)
+    base = jnp.asarray(np.kron(order[:count, :count], paley_signs()), jnp.bfloat16)
+    inner = jnp.asarray(sylvester(piece), jnp.bfloat16)
+    far_signs = order[first, ::count]
+    names = labels.start()
+    cut = [labels.split(*bit) for bit in stage.bits]
+    rest_names = [name for name in names if name not in cut]
+
+    def halves(values):
+        high = values.astype(jnp.bfloat16)
+        return high, (values - high.astype(jnp.float32)).astype(jnp.bfloat16)
+
+    def kernel(base_ref, inner_ref, *refs):
+        w_refs, refs = refs[:SPLIT], refs[SPLIT:]
+        outs, held, summed = refs[len(after):-2], refs[-2], refs[-1]
+        step = pl.program_id(0)
+        me = None if stage.kind == "all" else lax.axis_index("fsdp")
+
+        def gather(at, carry):
+            here = pl.multiple_of(at * 16, 16)
+            total = None
+            for far, sign in enumerate(far_signs):
+                part, inside = divmod(far * rows, rows_dev // SPLIT)
+                term = w_refs[part][pl.ds(here + inside, 16), :].astype(jnp.float32)
+                total = term if total is None else total + term if sign > 0 else total - term
+            summed[pl.ds(here, 16), :] = total
+            return carry
+
+        lax.fori_loop(0, rows // 16, gather, 0)
+        high, low = halves(summed[...])
+        turned = jnp.dot(base_ref[...], high, preferred_element_type=jnp.float32) + jnp.dot(
+            base_ref[...], low, preferred_element_type=jnp.float32
+        )
+        high, low = halves(turned)
+        turned = jnp.dot(high, inner_ref[...], preferred_element_type=jnp.float32) + jnp.dot(
+            low, inner_ref[...], preferred_element_type=jnp.float32
+        )
+        held[step] = turned
+
+        @pl.when(step == parts - 1)
+        def _():
+            before = [1.0 if me is None else parity_sign(a & me, parts) for a in range(parts)]
+
+            def body(at, carry):
+                here = pl.ds(pl.multiple_of(at * 8, 8), 8)
+                values = [held[a, here, :] for a in range(parts)]
+                if me is not None:
+                    values = [values[0]] + [before[a] * values[a] for a in range(1, parts)]
+                for j, value in enumerate(butterfly(values)):
+                    digits = values_of(names, j)
+                    targets = stage.views(outs, stage.fan, slot_of(rest_names, digits), here)
+                    targets[slot_of(cut, digits)][...] = value
+                return carry
+
+            lax.fori_loop(0, rows // 8, body, 0)
+
+    whole = lambda step: (0, 0)
+    slots = 1 << len(rest_names)
+    return pl.pallas_call(
+        kernel,
+        grid=(parts,),
+        in_specs=[
+            pl.BlockSpec((rows, rows), whole, pipeline_mode=pl.Buffered(1)),
+            pl.BlockSpec((piece, piece), whole, pipeline_mode=pl.Buffered(1)),
+        ]
+        + [
+            pl.BlockSpec((rows_dev // SPLIT, piece), functools.partial(lambda part, step: (part, step), part))
+            for part in range(SPLIT)
+        ]
+        + [ANYWHERE] * len(after),
+        out_specs=stage.blocks(slots, rows, piece, False),
+        out_shape=stage.shapes(slots, rows, piece),
+        scratch_shapes=[
+            pltpu.VMEM((parts, rows, piece), jnp.float32),
+            pltpu.VMEM((rows, piece), jnp.float32),
+        ],
+        compiler_params=compiler_params(48 * 2**20),
+        cost_estimate=TINY,
+        name="make_pieces",
+    )(base, inner, *[weight] * SPLIT, *after), rest_names
+
+
+def mix_pieces(arrays, names, came, going, labels, after, absolute):
+    rows, piece = arrays[0].shape[-2:]
+    made = [labels.made(*bit) for bit in came.bits]
+    cut = [labels.split(*bit) for bit in going.bits]
+    rest_names = [name for name in names + made if name not in cut]
+    slots_in, slots_out = 1 << len(names), 1 << len(rest_names)
+    strip, tile = 8, rows
+    for size in (104, 208):
+        if rows % size == 0:
+            tile = size
+
+    def kernel(*refs):
+        ins, outs = refs[: len(arrays)], refs[len(arrays) + len(after):]
+
+        def body(at, carry):
+            here = pl.ds(pl.multiple_of(at * strip, strip), strip)
+            for slot in range(slots_in):
+                values = came.values([view[...] for view in came.arrived(ins, slot, here)])
+                for w, value in enumerate(combine(came, made, values, absolute)):
+                    digits = {**values_of(names, slot), **values_of(made, w)}
+                    target = going.views(outs, going.fan, slot_of(rest_names, digits), here)
+                    if going.kind == "sum":
+                        index = slot_of(cut, digits) ^ going.place()
+                        outs[0][index, slot_of(rest_names, digits), here, :] = value
+                    else:
+                        target[slot_of(cut, digits)][...] = value
+            return carry
+
+        lax.fori_loop(0, tile // strip, body, 0)
+
+    return pl.pallas_call(
+        kernel,
+        grid=(rows // tile,),
+        in_specs=came.blocks(slots_in, tile, piece, True, True) + [ANYWHERE] * len(after),
+        out_specs=going.blocks(slots_out, tile, piece, True),
+        out_shape=going.shapes(slots_out, rows, piece),
+        compiler_params=compiler_params(24 * 2**20),
+        cost_estimate=TINY,
+        name="mix_pieces",
+    )(*arrays, *after), rest_names
+
+
+def finish(target, chunks, low, high, rows_slab, groups, labels, after):
+    piece = chunks[0][2][0].shape[-1]
+    each = 1 << labels.slab_bits
+    cols_out = groups * piece
+    cols_blocks = cols_out // BLOCK
+    blocks = [(m, b) for m in range(each) for b in range(low, high)]
+    needed = [c for c in chunks if c[0] < high * BLOCK and c[1] > low * BLOCK]
+    for c in needed:
+        assert c[3] == needed[0][3] and c[4].bits == needed[0][4].bits
+        assert c[4].kind == needed[0][4].kind
+    names, came = needed[0][3], needed[0][4]
+    made = [labels.made(*bit) for bit in came.bits]
+    factor = 1.0 / math.sqrt(FF * D)
+    operands = [array for c in needed for array in c[2]]
+    starts = np.cumsum([0] + [len(c[2]) for c in needed])
+    aliased = target is not None
+    per_block = {
+        b: [
+            (at, max(c[0], b * BLOCK), min(c[1], (b + 1) * BLOCK))
+            for at, c in enumerate(needed)
+            if max(c[0], b * BLOCK) < min(c[1], (b + 1) * BLOCK)
+        ]
+        for b in range(low, high)
+    }
+    most = max(len(s) for s in per_block.values())
+    slab_names = [name for name in names if name[0] == "m"]
+    column_names = [name for name in names if name[0] == "k"]
+    column_slots = 1 << len(column_names)
+
+    def kernel(*refs):
+        ins = refs[: len(operands)]
+        out, scales_ref, held, ready, in_sems, out_sems = refs[
+            len(operands) + int(aliased) + len(after):
+        ]
+        reads = []
+        for at, (m, b) in enumerate(blocks):
+            copies = []
+            for seg, (c, start, stop) in enumerate(per_block[b]):
+                base, sources = needed[c][0], ins[starts[c] : starts[c + 1]]
+                for column in range(column_slots):
+                    digits = {**values_of(slab_names, m), **values_of(column_names, column)}
+                    views = came.arrived(
+                        sources, slot_of(names, digits), pl.ds(start - base, stop - start)
+                    )
+                    for e, view in enumerate(views):
+                        copy = pltpu.make_async_copy(
+                            view,
+                            held.at[at, column, e, pl.ds(start - b * BLOCK, stop - start), :],
+                            in_sems.at[at, column, e, seg],
+                        )
+                        copy.start()
+                        copies.append(copy)
+            reads.append(copies)
+        lane = lax.broadcasted_iota(jnp.int32, (1, cols_blocks), 1)
+        writes = []
+        for at, (m, b) in enumerate(blocks):
+            for copy in reads[at]:
+                copy.wait()
+            found = jnp.zeros((1, cols_blocks), jnp.float32)
+            for part in range(piece // BLOCK):
+                span = pl.ds(part * BLOCK, BLOCK)
+                for column in range(column_slots):
+                    values = came.values([held[at, column, e, :, span] for e in range(came.fan)])
+                    values = [value * factor for value in values]
+                    for w, value in enumerate(combine(came, made, values)):
+                        digits = {**values_of(column_names, column), **values_of(made, w)}
+                        group = sum(bit << name[1] for name, bit in digits.items())
+                        top = jnp.max(
+                            jnp.max(jnp.abs(value), axis=0, keepdims=True), axis=1, keepdims=True
+                        )
+                        place = group * (piece // BLOCK) + part
+                        found = jnp.where(lane == place, top, found)
+                        ready[at, :, pl.ds(place * BLOCK, BLOCK)] = (
+                            value * (1.0 / (top + 1e-06))
+                        ).astype(jnp.bfloat16)
+            scales_ref[pl.ds(at, 1), :] = found
+            copy = pltpu.make_async_copy(
+                ready.at[at],
+                out.at[pl.ds(m * rows_slab + b * BLOCK, BLOCK), :],
+                out_sems.at[at],
+            )
+            copy.start()
+            writes.append(copy)
+        for copy in writes:
+            copy.wait()
+
+    total = len(blocks)
+    result, scales = pl.pallas_call(
+        kernel,
+        in_specs=[ANYWHERE] * (len(operands) + int(aliased) + len(after)),
+        out_specs=[ANYWHERE, pl.BlockSpec(memory_space=pltpu.VMEM)],
+        out_shape=[
+            jax.ShapeDtypeStruct((each * rows_slab, cols_out), jnp.bfloat16),
+            jax.ShapeDtypeStruct((total, cols_blocks), jnp.float32),
+        ],
+        scratch_shapes=[
+            pltpu.VMEM((total, column_slots, came.fan, BLOCK, piece), jnp.float32),
+            pltpu.VMEM((total, BLOCK, cols_out), jnp.bfloat16),
+            pltpu.SemaphoreType.DMA((total, column_slots, came.fan, most)),
+            pltpu.SemaphoreType.DMA((total,)),
+        ],
+        input_output_aliases={len(operands): 0} if aliased else {},
+        compiler_params=compiler_params(28 * 2**20),
+        cost_estimate=TINY,
+        name="finish",
+    )(*operands, *([target] if aliased else []), *after)
+    return result, scales.reshape(each, high - low, cols_blocks)
+
+
+def plan(sub_rows, labels):
+    every = [("fsdp", i) for i in range(labels.parts_bits)]
+    grp = [("grp", i) for i in range(labels.groups_bits)]
+    eighth = sub_rows // 8
+    sizes = [eighth // 2] * 2 + [eighth] * 7
+    chunks = [(size, [Stage("all", every), Stage("xor", grp)]) for size in sizes]
+    order = [0, 1]
+    for c in range(len(chunks)):
+        order += [c, c]
+        if c + 2 < len(chunks):
+            order += [c + 2]
+    return chunks, order
+
+
+def chunked_body(weight):
+    rows_dev, cols_dev = weight.shape
+    parts = lax.axis_size("fsdp")
+    groups = lax.axis_size("grp")
+    sub_rows = rows_dev // PALEY
+    labels = Labels(parts, groups)
+    chunks, order = plan(sub_rows, labels)
+    chained = CHAINED
+    firsts = np.cumsum([0] + [count for count, _ in chunks])
+    state = {}
+    result, scales, finished, token = None, [], [], ()
+    for c in order:
+        count, stages = chunks[c]
+        if c not in state:
+            arrays, names = make_pieces(
+                weight, int(firsts[c]), count, parts, token, stages[0], labels
+            )
+            token = (arrays[0],) if chained else ()
+            state[c] = (0, stages[0].send(arrays), names)
+            continue
+        at, arrays, names = state[c]
+        absolute = any(s.kind == "all" and s.bits[0][0] == "grp" for s in stages)
+        if at + 1 < len(stages):
+            arrays, names = mix_pieces(arrays, names, stages[at], stages[at + 1], labels, token, absolute)
+            token = (arrays[0],) if chained else ()
+            state[c] = (at + 1, stages[at + 1].send(arrays), names)
+            continue
+        low, high = int(firsts[c]) * PALEY, int(firsts[c + 1]) * PALEY
+        finished.append((low, high, arrays, names, stages[at]))
+        ready = [
+            b
+            for b in range(low // BLOCK, -(-high // BLOCK))
+            if sum(
+                max(0, min(f[1], (b + 1) * BLOCK) - max(f[0], b * BLOCK)) for f in finished
+            ) == BLOCK
+        ]
+        if ready:
+            result, found = finish(
+                result, finished, ready[0], ready[-1] + 1, rows_dev, groups, labels, token
+            )
+            token = (found,) if chained else ()
+            scales.append((ready[0], found))
+    scales = jnp.concatenate([found for _, found in sorted(scales, key=lambda s: s[0])], axis=1)
+    return result, scales.reshape(-1, scales.shape[-1])
+
+
+def body(weight):
+    rows_dev, cols_dev = weight.shape
+    parts = lax.axis_size("fsdp")
+    groups = lax.axis_size("grp")
+    tiled = (
+        cols_dev % (parts * LANES) == 0
+        and rows_dev % (8 * PALEY) == 0
+        and rows_dev % BLOCK == 0
+        and parts % groups == 0
+        and parts <= 8
+    )
+    return chunked_body(weight) if tiled else plain_body(weight)
+
+
 def solution(mesh):
     in_specs = (P("fsdp", "grp"),)
     out_specs = (P("grp", "fsdp"), P("grp", "fsdp"))

time: 1340 us -> 725 us (0.54)
  blocking collectives: 895 us -> 0 us
  waiting for transfers between devices: 0 us -> 437 us
  matrix products: 244 us -> 0 us
  Pallas kernels: 0 us -> 203 us
  local copies, waits for them, and re-layouts: 137 us -> 6.35 us
  starting transfers between devices: 0 us -> 74.7 us
  other arithmetic: 54.1 us -> 0 us
    all_to_all x2 -> x0, blocking collectives: 895 us -> none  [the longest x1 593 us: body(): lax.all_to_all(rotated, 'fsdp', split_axis=0, concat_axis=0, tiled=True)]
    ppermute x0 -> x27, waiting for transfers between devices: none -> 301 us  [send(): received.append(lax.ppermute(arrays[e], axis, pairs))]
    dot_general x6 -> x0, matrix products: 244 us -> none  [the longest x1 75.1 us: body(): jnp.einsum('qg,gmnaj->mnaqj', group_signs, moved, precision=exact_prec)]
    pallas_call x0 -> x27, Pallas kernels: none -> 203 us  [the longest x9 119 us: make_pieces(): pl.pallas_call(kernel, grid=(parts,), in_specs=[pl.BlockSpec((rows, rows)...]
    all_to_all x0 -> x9, waiting for transfers between devices: none -> 136 us  [send(): lax.all_to_all(arrays[0], self.bits[0][0], split_axis=0, concat_axis=0, t...]
    reshape x3 -> x6, local copies, waits for them, and re-layouts: 53.4 us -> 0.71 us  [the longest x1 0.67 us: chunked_body(): return (result, scales.reshape(-1, scales.shape[-1]))]
    all_to_all x0 -> x9, starting transfers between devices: none -> 47.4 us  [send(): lax.all_to_all(arrays[0], self.bits[0][0], split_axis=0, concat_axis=0, t...]
    unnamed x13 -> x82, local copies, waits for them, and re-layouts: 40.2 us -> 5.32 us
  transfers between devices with their start and end apart: 0 -> 36, of which waited for: 0 -> 33; matrix products, arithmetic and copies ran while one was open for 0% -> 0% of each run, Pallas kernels for 0% -> 25%
where the time goes in v1:
time: 725 us; the launch traced here: 723 us
  waiting for transfers between devices  437 us (60%)
  Pallas kernels  203 us (28%)
  starting transfers between devices  74.7 us (10%)
    ppermute x27, waiting for transfers between devices, send(): received.append(lax.ppermute(arrays[e], axis, pairs))  301 us
    all_to_all x9, waiting for transfers between devices, send(): lax.all_to_all(arrays[0], self.bits[0][0], split_axis=0, concat_axis=0, t...  136 us
    pallas_call x9, Pallas kernels, make_pieces(): pl.pallas_call(kernel, grid=(parts,), in_specs=[pl.BlockSpec((rows, rows)...  119 us
    pallas_call x9, Pallas kernels, finish(): pl.pallas_call(kernel, in_specs=[ANYWHERE] * (len(operands) + int(aliased...  57.7 us
    all_to_all x9, starting transfers between devices, send(): lax.all_to_all(arrays[0], self.bits[0][0], split_axis=0, concat_axis=0, t...  47.4 us
    ppermute x27, starting transfers between devices, send(): received.append(lax.ppermute(arrays[e], axis, pairs))  27.2 us
    pallas_call x9, Pallas kernels, mix_pieces(): pl.pallas_call(kernel, grid=(rows // tile,), in_specs=came.blocks(slots_i...  26.6 us
  transfers between devices with their start and end apart: 36, of which 33 were waited for; matrix products, arithmetic and copies ran while one was open for 0% of the time, Pallas kernels for 25%

profile of v1, /device:TPU:1, one launch (start us, length us, event | category | flops | bytes accessed | tf_op | source)
XLA Modules:
  0.0 722.8 jit_solution(6418903772975436233)
XLA Ops:
  31.6 27.6 %all-to-all-done.refs_0_ = f32[8,1,208,256]{3,2,1,0:T(8,128)S(1)} async-done(((f32[8,1,208,256]{3,2,1,0:T(8,128)}), f32[8,1,208,256]{3,2,1,0:T(8,128)S(1)}, u32[]{:S(2)}, u32[]{:S(2)}) %all-to-all-start) | async-done | bytes 1703968 | tf_op jit(solution)/shard_map/all_to_all | solution.py:179
  92.7 13.8 %make_pieces.11.refs_1_ = f32[8,1,416,256]{3,2,1,0:T(8,128)} custom-call(bf16[416,416]{1,0:T(8,128)(2,1)S(1)} %copy-done, bf16[256,256]{1,0:T(8,128)(2,1)S(1)} %copy-done.2, bf16[3328,2048]{1,0:T(8,128)(2,1)} %refs_1_.17, bf16[3328,2048]{1,0:T(8,128)(2,1)} %refs_1_.17, f32[2,1,8]{2,1,0:T(1,128)S(1)} %bitcast.12), custom_call_target="tpu_custom_call" | custom-call | tf_op jit(solution)/shard_map/make_pieces/pallas_call | solution.py:317
  139.2 13.7 %make_pieces.12.refs_1_ = f32[8,1,416,256]{3,2,1,0:T(8,128)} custom-call(bf16[416,416]{1,0:T(8,128)(2,1)S(1)} %copy-done, bf16[256,256]{1,0:T(8,128)(2,1)S(1)} %copy-done.2, bf16[3328,2048]{1,0:T(8,128)(2,1)} %refs_1_.17, bf16[3328,2048]{1,0:T(8,128)(2,1)} %refs_1_.17, f32[2,2,8]{2,1,0:T(2,128)S(1)} %bitcast.10), custom_call_target="tpu_custom_call" | custom-call | tf_op jit(solution)/shard_map/make_pieces/pallas_call | solution.py:317
  153.0 35.6 %all-to-all-done.1.refs_0_ = f32[8,1,416,256]{3,2,1,0:T(8,128)} async-done(((f32[8,1,416,256]{3,2,1,0:T(8,128)}), f32[8,1,416,256]{3,2,1,0:T(8,128)}, u32[]{:S(2)}, u32[]{:S(2)}) %all-to-all-start.1) | async-done | bytes 3407904 | tf_op jit(solution)/shard_map/all_to_all | solution.py:179
  199.9 18.6 %collective-permute-done.7.refs_6_.refs_2_ = f32[2,416,256]{2,1,0:T(8,128)S(1)} collective-permute-done((f32[2,416,256]{2,1,0:T(8,128)S(1)}, f32[2,416,256]{2,1,0:T(8,128)S(1)}, u32[]{:S(2)}, u32[]{:S(2)}) %collective-permute-start.7) | collective-permute-done | bytes 852000 | tf_op jit(solution)/shard_map/ppermute | solution.py:198
  218.5 18.7 %collective-permute-done.8.refs_7_.refs_3_ = f32[2,416,256]{2,1,0:T(8,128)S(1)} collective-permute-done((f32[2,416,256]{2,1,0:T(8,128)S(1)}, f32[2,416,256]{2,1,0:T(8,128)S(1)}, u32[]{:S(2)}, u32[]{:S(2)}) %collective-permute-start.8) | collective-permute-done | bytes 852000 | tf_op jit(solution)/shard_map/ppermute | solution.py:198
  243.9 13.7 %make_pieces.13.refs_1_ = f32[8,1,416,256]{3,2,1,0:T(8,128)} custom-call(bf16[416,416]{1,0:T(8,128)(2,1)S(1)} %copy-done, bf16[256,256]{1,0:T(8,128)(2,1)S(1)} %copy-done.2, bf16[3328,2048]{1,0:T(8,128)(2,1)} %refs_1_.17, bf16[3328,2048]{1,0:T(8,128)(2,1)} %refs_1_.17, f32[2,3,8]{2,1,0:T(4,128)S(1)} %reshape.36.refs_2_), custom_call_target="tpu_custom_call" | custom-call | tf_op jit(solution)/shard_map/make_pieces/pallas_call | solution.py:317
  280.7 18.6 %collective-permute-done.10.refs_6_.refs_2_ = f32[2,416,256]{2,1,0:T(8,128)S(1)} collective-permute-done((f32[2,416,256]{2,1,0:T(8,128)S(1)}, f32[2,416,256]{2,1,0:T(8,128)S(1)}, u32[]{:S(2)}, u32[]{:S(2)}) %collective-permute-start.10) | collective-permute-done | bytes 852000 | tf_op jit(solution)/shard_map/ppermute | solution.py:198
  299.3 18.7 %collective-permute-done.11.refs_7_.refs_3_ = f32[2,416,256]{2,1,0:T(8,128)S(1)} collective-permute-done((f32[2,416,256]{2,1,0:T(8,128)S(1)}, f32[2,416,256]{2,1,0:T(8,128)S(1)}, u32[]{:S(2)}, u32[]{:S(2)}) %collective-permute-start.11) | collective-permute-done | bytes 852000 | tf_op jit(solution)/shard_map/ppermute | solution.py:198
  324.8 13.8 %make_pieces.14.refs_1_ = f32[8,1,416,256]{3,2,1,0:T(8,128)} custom-call(bf16[416,416]{1,0:T(8,128)(2,1)S(1)} %copy-done, bf16[256,256]{1,0:T(8,128)(2,1)S(1)} %copy-done.2, bf16[3328,2048]{1,0:T(8,128)(2,1)} %refs_1_.17, bf16[3328,2048]{1,0:T(8,128)(2,1)} %refs_1_.17, f32[2,3,8]{2,1,0:T(4,128)S(1)} %reshape.37.refs_2_), custom_call_target="tpu_custom_call" | custom-call | tf_op jit(solution)/shard_map/make_pieces/pallas_call | solution.py:317
  360.9 18.6 %collective-permute-done.13.refs_6_ = f32[2,416,256]{2,1,0:T(8,128)S(1)} collective-permute-done((f32[2,416,256]{2,1,0:T(8,128)S(1)}, f32[2,416,256]{2,1,0:T(8,128)S(1)}, u32[]{:S(2)}, u32[]{:S(2)}) %collective-permute-start.13) | collective-permute-done | bytes 852000 | tf_op jit(solution)/shard_map/ppermute | solution.py:198
  379.6 18.7 %collective-permute-done.14.refs_7_ = f32[2,416,256]{2,1,0:T(8,128)S(1)} collective-permute-done((f32[2,416,256]{2,1,0:T(8,128)S(1)}, f32[2,416,256]{2,1,0:T(8,128)S(1)}, u32[]{:S(2)}, u32[]{:S(2)}) %collective-permute-start.14) | collective-permute-done | bytes 852000 | tf_op jit(solution)/shard_map/ppermute | solution.py:198
  406.9 13.8 %make_pieces.15.refs_1_ = f32[8,1,416,256]{3,2,1,0:T(8,128)} custom-call(bf16[416,416]{1,0:T(8,128)(2,1)S(1)} %copy-done, bf16[256,256]{1,0:T(8,128)(2,1)S(1)} %copy-done.2, bf16[3328,2048]{1,0:T(8,128)(2,1)} %refs_1_.17, bf16[3328,2048]{1,0:T(8,128)(2,1)} %refs_1_.17, f32[2,4,8]{2,1,0:T(4,128)S(1)} %bitcast.8), custom_call_target="tpu_custom_call" | custom-call | tf_op jit(solution)/shard_map/make_pieces/pallas_call | solution.py:317
  441.2 18.6 %collective-permute-done.16.refs_2_ = f32[2,416,256]{2,1,0:T(8,128)S(1)} collective-permute-done((f32[2,416,256]{2,1,0:T(8,128)S(1)}, f32[2,416,256]{2,1,0:T(8,128)S(1)}, u32[]{:S(2)}, u32[]{:S(2)}) %collective-permute-start.16) | collective-permute-done | bytes 852000 | tf_op jit(solution)/shard_map/ppermute | solution.py:198
  459.8 18.7 %collective-permute-done.17.refs_3_ = f32[2,416,256]{2,1,0:T(8,128)S(1)} collective-permute-done((f32[2,416,256]{2,1,0:T(8,128)S(1)}, f32[2,416,256]{2,1,0:T(8,128)S(1)}, u32[]{:S(2)}, u32[]{:S(2)}) %collective-permute-start.17) | collective-permute-done | bytes 852000 | tf_op jit(solution)/shard_map/ppermute | solution.py:198
  485.0 13.7 %make_pieces.16.refs_1_ = f32[8,1,416,256]{3,2,1,0:T(8,128)} custom-call(bf16[416,416]{1,0:T(8,128)(2,1)S(1)} %copy-done, bf16[256,256]{1,0:T(8,128)(2,1)S(1)} %copy-done.2, bf16[3328,2048]{1,0:T(8,128)(2,1)} %refs_1_.17, bf16[3328,2048]{1,0:T(8,128)(2,1)} %refs_1_.17, f32[2,3,8]{2,1,0:T(4,128)S(1)} %reshape.39.refs_2_), custom_call_target="tpu_custom_call" | custom-call | tf_op jit(solution)/shard_map/make_pieces/pallas_call | solution.py:317
  521.6 18.6 %collective-permute-done.19.refs_6_.refs_2_ = f32[2,416,256]{2,1,0:T(8,128)S(1)} collective-permute-done((f32[2,416,256]{2,1,0:T(8,128)S(1)}, f32[2,416,256]{2,1,0:T(8,128)S(1)}, u32[]{:S(2)}, u32[]{:S(2)}) %collective-permute-start.19) | collective-permute-done | bytes 852000 | tf_op jit(solution)/shard_map/ppermute | solution.py:198
  540.2 18.7 %collective-permute-done.20.refs_7_.refs_3_ = f32[2,416,256]{2,1,0:T(8,128)S(1)} collective-permute-done((f32[2,416,256]{2,1,0:T(8,128)S(1)}, f32[2,416,256]{2,1,0:T(8,128)S(1)}, u32[]{:S(2)}, u32[]{:S(2)}) %collective-permute-start.20) | collective-permute-done | bytes 852000 | tf_op jit(solution)/shard_map/ppermute | solution.py:198
  565.6 13.7 %make_pieces.17.refs_1_ = f32[8,1,416,256]{3,2,1,0:T(8,128)} custom-call(bf16[416,416]{1,0:T(8,128)(2,1)S(1)} %copy-done, bf16[256,256]{1,0:T(8,128)(2,1)S(1)} %copy-done.2, bf16[3328,2048]{1,0:T(8,128)(2,1)} %refs_1_.17, bf16[3328,2048]{1,0:T(8,128)(2,1)} %refs_1_.17, f32[2,3,8]{2,1,0:T(4,128)S(1)} %reshape.40.refs_2_), custom_call_target="tpu_custom_call" | custom-call | tf_op jit(solution)/shard_map/make_pieces/pallas_call | solution.py:317
  601.1 18.5 %collective-permute-done.22.refs_6_.refs_2_ = f32[2,416,256]{2,1,0:T(8,128)S(1)} collective-permute-done((f32[2,416,256]{2,1,0:T(8,128)S(1)}, f32[2,416,256]{2,1,0:T(8,128)S(1)}, u32[]{:S(2)}, u32[]{:S(2)}) %collective-permute-start.22) | collective-permute-done | bytes 852000 | tf_op jit(solution)/shard_map/ppermute | solution.py:198
  619.6 18.7 %collective-permute-done.23.refs_7_.refs_3_ = f32[2,416,256]{2,1,0:T(8,128)S(1)} collective-permute-done((f32[2,416,256]{2,1,0:T(8,128)S(1)}, f32[2,416,256]{2,1,0:T(8,128)S(1)}, u32[]{:S(2)}, u32[]{:S(2)}) %collective-permute-start.23) | collective-permute-done | bytes 852000 | tf_op jit(solution)/shard_map/ppermute | solution.py:198
  645.1 24.9 %all-to-all-done.8.refs_0_ = f32[8,1,416,256]{3,2,1,0:T(8,128)S(1)} async-done(((f32[8,1,416,256]{3,2,1,0:T(8,128)}), f32[8,1,416,256]{3,2,1,0:T(8,128)S(1)}, u32[]{:S(2)}, u32[]{:S(2)}) %all-to-all-start.8) | async-done | bytes 3407904 | tf_op jit(solution)/shard_map/all_to_all | solution.py:179
  676.2 18.5 %collective-permute-done.25.refs_6_ = f32[2,416,256]{2,1,0:T(8,128)S(1)} collective-permute-done((f32[2,416,256]{2,1,0:T(8,128)S(1)}, f32[2,416,256]{2,1,0:T(8,128)S(1)}, u32[]{:S(2)}, u32[]{:S(2)}) %collective-permute-start.25) | collective-permute-done | bytes 852000 | tf_op jit(solution)/shard_map/ppermute | solution.py:198
  694.7 18.4 %collective-permute-done.26.refs_7_ = f32[2,416,256]{2,1,0:T(8,128)S(1)} collective-permute-done((f32[2,416,256]{2,1,0:T(8,128)S(1)}, f32[2,416,256]{2,1,0:T(8,128)S(1)}, u32[]{:S(2)}, u32[]{:S(2)}) %collective-permute-start.26) | collective-permute-done | bytes 852000 | tf_op jit(solution)/shard_map/ppermute | solution.py:198
  (165 shorter events, 276.4 us)
Async XLA Ops:
  13.8 45.5 %all-to-all-start = ((f32[8,1,208,256]{3,2,1,0:T(8,128)}), f32[8,1,208,256]{3,2,1,0:T(8,128)S(1)}, u32[]{:S(2)}, u32[]{:S(2)}) async-start(f32[8,1,208,256]{3,2,1,0:T(8,128)} %make_pieces.9.refs_2_), calls=%async_computation | async-start | bytes 3407872 | tf_op jit(solution)/shard_map/all_to_all | solution.py:179
  60.4 46.0 %all-to-all-start.2 = ((f32[8,1,208,256]{3,2,1,0:T(8,128)}), f32[8,1,208,256]{3,2,1,0:T(8,128)S(1)}, u32[]{:S(2)}, u32[]{:S(2)}) async-start(f32[8,1,208,256]{3,2,1,0:T(8,128)} %make_pieces.10.refs_1_), calls=%async_computation.2 | async-start | bytes 3407872 | tf_op jit(solution)/shard_map/all_to_all | solution.py:179
  106.4 82.1 %all-to-all-start.1 = ((f32[8,1,416,256]{3,2,1,0:T(8,128)}), f32[8,1,416,256]{3,2,1,0:T(8,128)}, u32[]{:S(2)}, u32[]{:S(2)}) async-start(f32[8,1,416,256]{3,2,1,0:T(8,128)} %make_pieces.11.refs_1_), calls=%async_computation.1 | async-start | bytes 6815744 | tf_op jit(solution)/shard_map/all_to_all | solution.py:179
  114.6 19.9 %collective-permute-start.5 = (f32[2,208,256]{2,1,0:T(8,128)S(1)}, f32[2,208,256]{2,1,0:T(8,128)S(1)}, u32[]{:S(2)}, u32[]{:S(2)}) collective-permute-start(f32[2,208,256]{2,1,0:T(8,128)S(1)} %get-tuple-element.64), channel_id=1, source_target_pairs={{0,3},{1,2},{2,1},{3,0},{4,7},{5,6},{6,5},{7,4},{8,11},{9,10},{10,... | collective-permute-start | bytes 1277960 | tf_op jit(solution)/shard_map/ppermute | solution.py:198
  188.5 79.9 %all-to-all-start.3 = ((f32[8,1,416,256]{3,2,1,0:T(8,128)}), f32[8,1,416,256]{3,2,1,0:T(8,128)}, u32[]{:S(2)}, u32[]{:S(2)}) async-start(f32[8,1,416,256]{3,2,1,0:T(8,128)} %make_pieces.12.refs_1_), calls=%async_computation.3 | async-start | bytes 6815744 | tf_op jit(solution)/shard_map/all_to_all | solution.py:179
  197.8 20.6 %collective-permute-start.7 = (f32[2,416,256]{2,1,0:T(8,128)S(1)}, f32[2,416,256]{2,1,0:T(8,128)S(1)}, u32[]{:S(2)}, u32[]{:S(2)}) collective-permute-start(f32[2,416,256]{2,1,0:T(8,128)S(1)} %get-tuple-element.69), channel_id=1, source_target_pairs={{0,2},{1,3},{2,0},{3,1},{4,6},{5,7},{6,4},{7,5},{8,10},{9,11},{10,... | collective-permute-start | bytes 2555912 | tf_op jit(solution)/shard_map/ppermute | solution.py:198
  199.1 38.1 %collective-permute-start.8 = (f32[2,416,256]{2,1,0:T(8,128)S(1)}, f32[2,416,256]{2,1,0:T(8,128)S(1)}, u32[]{:S(2)}, u32[]{:S(2)}) collective-permute-start(f32[2,416,256]{2,1,0:T(8,128)S(1)} %get-tuple-element.70), channel_id=1, source_target_pairs={{0,3},{1,2},{2,1},{3,0},{4,7},{5,6},{6,5},{7,4},{8,11},{9,10},{10,... | collective-permute-start | bytes 2555912 | tf_op jit(solution)/shard_map/ppermute | solution.py:198
  268.4 79.7 %all-to-all-start.5 = ((f32[8,1,416,256]{3,2,1,0:T(8,128)}), f32[8,1,416,256]{3,2,1,0:T(8,128)}, u32[]{:S(2)}, u32[]{:S(2)}) async-start(f32[8,1,416,256]{3,2,1,0:T(8,128)} %make_pieces.13.refs_1_), calls=%async_computation.5 | async-start | bytes 6815744 | tf_op jit(solution)/shard_map/all_to_all | solution.py:179
  278.7 20.6 %collective-permute-start.10 = (f32[2,416,256]{2,1,0:T(8,128)S(1)}, f32[2,416,256]{2,1,0:T(8,128)S(1)}, u32[]{:S(2)}, u32[]{:S(2)}) collective-permute-start(f32[2,416,256]{2,1,0:T(8,128)S(1)} %get-tuple-element.75), channel_id=1, source_target_pairs={{0,2},{1,3},{2,0},{3,1},{4,6},{5,7},{6,4},{7,5},{8,10},{9,11},{10,... | collective-permute-start | bytes 2555912 | tf_op jit(solution)/shard_map/ppermute | solution.py:198
  279.9 38.1 %collective-permute-start.11 = (f32[2,416,256]{2,1,0:T(8,128)S(1)}, f32[2,416,256]{2,1,0:T(8,128)S(1)}, u32[]{:S(2)}, u32[]{:S(2)}) collective-permute-start(f32[2,416,256]{2,1,0:T(8,128)S(1)} %get-tuple-element.76), channel_id=1, source_target_pairs={{0,3},{1,2},{2,1},{3,0},{4,7},{5,6},{6,5},{7,4},{8,11},{9,10},{10,... | collective-permute-start | bytes 2555912 | tf_op jit(solution)/shard_map/ppermute | solution.py:198
  348.2 80.2 %all-to-all-start.4 = ((f32[8,1,416,256]{3,2,1,0:T(8,128)}), f32[8,1,416,256]{3,2,1,0:T(8,128)}, u32[]{:S(2)}, u32[]{:S(2)}) async-start(f32[8,1,416,256]{3,2,1,0:T(8,128)} %make_pieces.14.refs_1_), calls=%async_computation.4 | async-start | bytes 6815744 | tf_op jit(solution)/shard_map/all_to_all | solution.py:179
  358.9 20.6 %collective-permute-start.13 = (f32[2,416,256]{2,1,0:T(8,128)S(1)}, f32[2,416,256]{2,1,0:T(8,128)S(1)}, u32[]{:S(2)}, u32[]{:S(2)}) collective-permute-start(f32[2,416,256]{2,1,0:T(8,128)S(1)} %get-tuple-element.81), channel_id=1, source_target_pairs={{0,2},{1,3},{2,0},{3,1},{4,6},{5,7},{6,4},{7,5},{8,10},{9,11},{10,... | collective-permute-start | bytes 2555912 | tf_op jit(solution)/shard_map/ppermute | solution.py:198
  360.1 38.1 %collective-permute-start.14 = (f32[2,416,256]{2,1,0:T(8,128)S(1)}, f32[2,416,256]{2,1,0:T(8,128)S(1)}, u32[]{:S(2)}, u32[]{:S(2)}) collective-permute-start(f32[2,416,256]{2,1,0:T(8,128)S(1)} %get-tuple-element.82), channel_id=1, source_target_pairs={{0,3},{1,2},{2,1},{3,0},{4,7},{5,6},{6,5},{7,4},{8,11},{9,10},{10,... | collective-permute-start | bytes 2555912 | tf_op jit(solution)/shard_map/ppermute | solution.py:198
  428.4 80.4 %all-to-all-start.7 = ((f32[8,1,416,256]{3,2,1,0:T(8,128)}), f32[8,1,416,256]{3,2,1,0:T(8,128)}, u32[]{:S(2)}, u32[]{:S(2)}) async-start(f32[8,1,416,256]{3,2,1,0:T(8,128)} %make_pieces.15.refs_1_), calls=%async_computation.7 | async-start | bytes 6815744 | tf_op jit(solution)/shard_map/all_to_all | solution.py:179
  439.2 20.6 %collective-permute-start.16 = (f32[2,416,256]{2,1,0:T(8,128)S(1)}, f32[2,416,256]{2,1,0:T(8,128)S(1)}, u32[]{:S(2)}, u32[]{:S(2)}) collective-permute-start(f32[2,416,256]{2,1,0:T(8,128)S(1)} %get-tuple-element.87), channel_id=1, source_target_pairs={{0,2},{1,3},{2,0},{3,1},{4,6},{5,7},{6,4},{7,5},{8,10},{9,11},{10,... | collective-permute-start | bytes 2555912 | tf_op jit(solution)/shard_map/ppermute | solution.py:198
  440.4 38.1 %collective-permute-start.17 = (f32[2,416,256]{2,1,0:T(8,128)S(1)}, f32[2,416,256]{2,1,0:T(8,128)S(1)}, u32[]{:S(2)}, u32[]{:S(2)}) collective-permute-start(f32[2,416,256]{2,1,0:T(8,128)S(1)} %get-tuple-element.88), channel_id=1, source_target_pairs={{0,3},{1,2},{2,1},{3,0},{4,7},{5,6},{6,5},{7,4},{8,11},{9,10},{10,... | collective-permute-start | bytes 2555912 | tf_op jit(solution)/shard_map/ppermute | solution.py:198
  508.9 80.2 %all-to-all-start.6 = ((f32[8,1,416,256]{3,2,1,0:T(8,128)}), f32[8,1,416,256]{3,2,1,0:T(8,128)}, u32[]{:S(2)}, u32[]{:S(2)}) async-start(f32[8,1,416,256]{3,2,1,0:T(8,128)} %make_pieces.16.refs_1_), calls=%async_computation.6 | async-start | bytes 6815744 | tf_op jit(solution)/shard_map/all_to_all | solution.py:179
  519.6 20.6 %collective-permute-start.19 = (f32[2,416,256]{2,1,0:T(8,128)S(1)}, f32[2,416,256]{2,1,0:T(8,128)S(1)}, u32[]{:S(2)}, u32[]{:S(2)}) collective-permute-start(f32[2,416,256]{2,1,0:T(8,128)S(1)} %get-tuple-element.93), channel_id=1, source_target_pairs={{0,2},{1,3},{2,0},{3,1},{4,6},{5,7},{6,4},{7,5},{8,10},{9,11},{10,... | collective-permute-start | bytes 2555912 | tf_op jit(solution)/shard_map/ppermute | solution.py:198
  520.8 38.1 %collective-permute-start.20 = (f32[2,416,256]{2,1,0:T(8,128)S(1)}, f32[2,416,256]{2,1,0:T(8,128)S(1)}, u32[]{:S(2)}, u32[]{:S(2)}) collective-permute-start(f32[2,416,256]{2,1,0:T(8,128)S(1)} %get-tuple-element.94), channel_id=1, source_target_pairs={{0,3},{1,2},{2,1},{3,0},{4,7},{5,6},{6,5},{7,4},{8,11},{9,10},{10,... | collective-permute-start | bytes 2555912 | tf_op jit(solution)/shard_map/ppermute | solution.py:198
  589.1 81.0 %all-to-all-start.8 = ((f32[8,1,416,256]{3,2,1,0:T(8,128)}), f32[8,1,416,256]{3,2,1,0:T(8,128)S(1)}, u32[]{:S(2)}, u32[]{:S(2)}) async-start(f32[8,1,416,256]{3,2,1,0:T(8,128)} %make_pieces.17.refs_1_), calls=%async_computation.8 | async-start | bytes 6815744 | tf_op jit(solution)/shard_map/all_to_all | solution.py:179
  599.1 20.5 %collective-permute-start.22 = (f32[2,416,256]{2,1,0:T(8,128)S(1)}, f32[2,416,256]{2,1,0:T(8,128)S(1)}, u32[]{:S(2)}, u32[]{:S(2)}) collective-permute-start(f32[2,416,256]{2,1,0:T(8,128)S(1)} %get-tuple-element.99), channel_id=1, source_target_pairs={{0,2},{1,3},{2,0},{3,1},{4,6},{5,7},{6,4},{7,5},{8,10},{9,11},{10,... | collective-permute-start | bytes 2555912 | tf_op jit(solution)/shard_map/ppermute | solution.py:198
  600.3 38.0 %collective-permute-start.23 = (f32[2,416,256]{2,1,0:T(8,128)S(1)}, f32[2,416,256]{2,1,0:T(8,128)S(1)}, u32[]{:S(2)}, u32[]{:S(2)}) collective-permute-start(f32[2,416,256]{2,1,0:T(8,128)S(1)} %get-tuple-element.100), channel_id=1, source_target_pairs={{0,3},{1,2},{2,1},{3,0},{4,7},{5,6},{6,5},{7,4},{8,11},{9,10},{10,... | collective-permute-start | bytes 2555912 | tf_op jit(solution)/shard_map/ppermute | solution.py:198
  674.2 20.5 %collective-permute-start.25 = (f32[2,416,256]{2,1,0:T(8,128)S(1)}, f32[2,416,256]{2,1,0:T(8,128)S(1)}, u32[]{:S(2)}, u32[]{:S(2)}) collective-permute-start(f32[2,416,256]{2,1,0:T(8,128)S(1)} %get-tuple-element.105), channel_id=1, source_target_pairs={{0,2},{1,3},{2,0},{3,1},{4,6},{5,7},{6,4},{7,5},{8,10},{9,11},{10,... | collective-permute-start | bytes 2555912 | tf_op jit(solution)/shard_map/ppermute | solution.py:198
  675.4 37.7 %collective-permute-start.26 = (f32[2,416,256]{2,1,0:T(8,128)S(1)}, f32[2,416,256]{2,1,0:T(8,128)S(1)}, u32[]{:S(2)}, u32[]{:S(2)}) collective-permute-start(f32[2,416,256]{2,1,0:T(8,128)S(1)} %get-tuple-element.106), channel_id=1, source_target_pairs={{0,3},{1,2},{2,1},{3,0},{4,7},{5,6},{6,5},{7,4},{8,11},{9,10},{10,... | collective-permute-start | bytes 2555912 | tf_op jit(solution)/shard_map/ppermute | solution.py:198
  (53 other events, 1215.0 us)

commit v2 on v1

--- a/solution.py
+++ b/solution.py
@@ -15,7 +15,6 @@
 PALEY = 52
 LANES = 128
 SPLIT = 2
-CHAINED = True
 
 
 def paley_signs():
@@ -140,6 +139,7 @@
 
 
 TINY = pl.CostEstimate(flops=0, bytes_accessed=0, transcendentals=0)
+LONG = pl.CostEstimate(flops=10**12, bytes_accessed=4 * 10**9, transcendentals=0)
 ANYWHERE = pl.BlockSpec(memory_space=pl.ANY)
 
 
@@ -483,7 +483,7 @@
         ],
         input_output_aliases={len(operands): 0} if aliased else {},
         compiler_params=compiler_params(28 * 2**20),
-        cost_estimate=TINY,
+        cost_estimate=LONG,
         name="finish",
     )(*operands, *([target] if aliased else []), *after)
     return result, scales.reshape(each, high - low, cols_blocks)
@@ -492,15 +492,18 @@
 def plan(sub_rows, labels):
     every = [("fsdp", i) for i in range(labels.parts_bits)]
     grp = [("grp", i) for i in range(labels.groups_bits)]
-    eighth = sub_rows // 8
-    sizes = [eighth // 2] * 2 + [eighth] * 7
-    chunks = [(size, [Stage("all", every), Stage("xor", grp)]) for size in sizes]
+    unit = sub_rows // 16
+    stages = [Stage("all", every), Stage("xor", grp)]
+    chunks = [(unit * times, stages) for times in (1, 1, 2, 4, 4, 2, 1, 1)]
+    n = len(chunks)
     order = [0, 1]
-    for c in range(len(chunks)):
-        order += [c, c]
-        if c + 2 < len(chunks):
+    for c in range(n):
+        if c >= 1 and c < n - 1:
+            order += [c - 1]
+        order += [c]
+        if c + 2 < n:
             order += [c + 2]
-    return chunks, order
+    return chunks, order + [n - 2, n - 1]
 
 
 def chunked_body(weight):
@@ -510,7 +513,6 @@
     sub_rows = rows_dev // PALEY
     labels = Labels(parts, groups)
     chunks, order = plan(sub_rows, labels)
-    chained = CHAINED
     firsts = np.cumsum([0] + [count for count, _ in chunks])
     state = {}
     result, scales, finished, token = None, [], [], ()
@@ -520,14 +522,14 @@
             arrays, names = make_pieces(
                 weight, int(firsts[c]), count, parts, token, stages[0], labels
             )
-            token = (arrays[0],) if chained else ()
+            token = (arrays[0],)
             state[c] = (0, stages[0].send(arrays), names)
             continue
         at, arrays, names = state[c]
         absolute = any(s.kind == "all" and s.bits[0][0] == "grp" for s in stages)
         if at + 1 < len(stages):
             arrays, names = mix_pieces(arrays, names, stages[at], stages[at + 1], labels, token, absolute)
-            token = (arrays[0],) if chained else ()
+            token = (arrays[0],)
             state[c] = (at + 1, stages[at + 1].send(arrays), names)
             continue
         low, high = int(firsts[c]) * PALEY, int(firsts[c + 1]) * PALEY
@@ -543,7 +545,7 @@
             result, found = finish(
                 result, finished, ready[0], ready[-1] + 1, rows_dev, groups, labels, token
             )
-            token = (found,) if chained else ()
+            token = (found,)
             scales.append((ready[0], found))
     scales = jnp.concatenate([found for _, found in sorted(scales, key=lambda s: s[0])], axis=1)
     return result, scales.reshape(-1, scales.shape[-1])

time: 725 us -> 694 us (0.957)
  waiting for transfers between devices: 437 us -> 416 us
  Pallas kernels: 203 us -> 190 us
  local copies, waits for them, and re-layouts: 6.35 us -> 17.4 us
  starting transfers between devices: 74.7 us -> 67.3 us
    ppermute x27 -> x24, waiting for transfers between devices: 301 us -> 50.7 us  [send(): received.append(lax.ppermute(arrays[e], axis, pairs))]
    all_to_all x9 -> x8, waiting for transfers between devices: 136 us -> 365 us  [send(): lax.all_to_all(arrays[0], self.bits[0][0], split_axis=0, concat_axis=0, t...]
    pallas_call x9 -> x8, Pallas kernels: 57.7 us -> 37.9 us  [finish(): pl.pallas_call(kernel, in_specs=[ANYWHERE] * (len(operands) + int(aliased...]
    pallas_call x9 -> x8, Pallas kernels: 26.6 us -> 35.2 us  [mix_pieces(): pl.pallas_call(kernel, grid=(rows // tile,), in_specs=came.blocks(slots_i...]
    unnamed x82 -> x78, local copies, waits for them, and re-layouts: 5.32 us -> 12.6 us
    all_to_all x9 -> x8, starting transfers between devices: 47.4 us -> 42.6 us  [send(): lax.all_to_all(arrays[0], self.bits[0][0], split_axis=0, concat_axis=0, t...]
    ppermute x27 -> x24, starting transfers between devices: 27.2 us -> 24.6 us  [send(): received.append(lax.ppermute(arrays[e], axis, pairs))]
    pallas_call x9 -> x8, Pallas kernels: 119 us -> 117 us  [make_pieces(): pl.pallas_call(kernel, grid=(parts,), in_specs=[pl.BlockSpec((rows, rows)...]
  transfers between devices with their start and end apart: 36 -> 32, of which waited for: 33 -> 14; matrix products, arithmetic and copies ran while one was open for 0% -> 1% of each run, Pallas kernels for 25% -> 25%
where the time goes in v2:
time: 694 us; the launch traced here: 692 us
  waiting for transfers between devices  416 us (60%)
  Pallas kernels  190 us (27%)
  starting transfers between devices  67.3 us (10%)
  local copies, waits for them, and re-layouts  17.4 us (3%)
    all_to_all x8, waiting for transfers between devices, send(): lax.all_to_all(arrays[0], self.bits[0][0], split_axis=0, concat_axis=0, t...  365 us
    pallas_call x8, Pallas kernels, make_pieces(): pl.pallas_call(kernel, grid=(parts,), in_specs=[pl.BlockSpec((rows, rows)...  117 us
    ppermute x24, waiting for transfers between devices, send(): received.append(lax.ppermute(arrays[e], axis, pairs))  50.7 us
    all_to_all x8, starting transfers between devices, send(): lax.all_to_all(arrays[0], self.bits[0][0], split_axis=0, concat_axis=0, t...  42.6 us
    pallas_call x8, Pallas kernels, finish(): pl.pallas_call(kernel, in_specs=[ANYWHERE] * (len(operands) + int(aliased...  37.9 us
    pallas_call x8, Pallas kernels, mix_pieces(): pl.pallas_call(kernel, grid=(rows // tile,), in_specs=came.blocks(slots_i...  35.2 us
    ppermute x24, starting transfers between devices, send(): received.append(lax.ppermute(arrays[e], axis, pairs))  24.6 us
  transfers between devices with their start and end apart: 32, of which 14 were waited for; matrix products, arithmetic and copies ran while one was open for 1% of the time, Pallas kernels for 25%

profile of v2, /device:TPU:1, one launch (start us, length us, event | category | flops | bytes accessed | tf_op | source)
XLA Modules:
  0.0 691.7 jit_solution(5894384314504603442)
XLA Ops:
  2.4 11.3 %make_pieces.8.refs_2_ = f32[8,1,208,256]{3,2,1,0:T(8,128)} custom-call(bf16[208,208]{1,0:T(8,128)(2,1)S(1)} %copy-done.6, bf16[256,256]{1,0:T(8,128)(2,1)S(1)} %copy-done.2, bf16[3328,2048]{1,0:T(8,128)(2,1)} %refs_1_.15, bf16[3328,2048]{1,0:T(8,128)(2,1)} %refs_1_.15), custom_call_target="tpu_custom_call" | custom-call | tf_op jit(solution)/shard_map/make_pieces/pallas_call | solution.py:317
  13.8 6.5 all-to-all-start
  20.3 11.4 %make_pieces.9.refs_1_ = f32[8,1,208,256]{3,2,1,0:T(8,128)} custom-call(bf16[208,208]{1,0:T(8,128)(2,1)S(1)} %copy-done.7, bf16[256,256]{1,0:T(8,128)(2,1)S(1)} %copy-done.3, bf16[3328,2048]{1,0:T(8,128)(2,1)} %refs_1_.15, bf16[3328,2048]{1,0:T(8,128)(2,1)} %refs_1_.15, f32[8,1,208,256]{3,2,1,0:T(8,128)} %make_pieces.8.refs_2_), custom_call_target="tpu_custom_call" | custom-call | tf_op jit(solution)/shard_map/make_pieces/pallas_call | solution.py:317
  31.7 27.6 %all-to-all-done.refs_0_ = f32[8,1,208,256]{3,2,1,0:T(8,128)S(1)} async-done(((f32[8,1,208,256]{3,2,1,0:T(8,128)}), f32[8,1,208,256]{3,2,1,0:T(8,128)S(1)}, u32[]{:S(2)}, u32[]{:S(2)}) %all-to-all-start) | async-done | bytes 1703968 | tf_op jit(solution)/shard_map/all_to_all | solution.py:179
  68.3 13.8 %make_pieces.10.refs_4_ = f32[8,1,416,256]{3,2,1,0:T(8,128)} custom-call(bf16[416,416]{1,0:T(8,128)(2,1)S(1)} %copy-done.10, bf16[256,256]{1,0:T(8,128)(2,1)S(1)} %copy-done.3, bf16[3328,2048]{1,0:T(8,128)(2,1)} %refs_1_.15, bf16[3328,2048]{1,0:T(8,128)(2,1)} %refs_1_.15, f32[2,208,256]{2,1,0:T(8,128)S(1)} %get-tuple-element.50.refs_2_.refs_0_), custom_call_target="tpu_custom_call" | custom-call | tf_op jit(solution)/shard_map/make_pieces/pallas_call | solution.py:317
  82.9 20.2 %all-to-all-done.2.refs_0_ = f32[8,1,208,256]{3,2,1,0:T(8,128)S(1)} async-done(((f32[8,1,208,256]{3,2,1,0:T(8,128)}), f32[8,1,208,256]{3,2,1,0:T(8,128)S(1)}, u32[]{:S(2)}, u32[]{:S(2)}) %all-to-all-start.2) | async-done | bytes 1703968 | tf_op jit(solution)/shard_map/all_to_all | solution.py:179
  115.7 22.1 %make_pieces.11.refs_9_ = f32[8,1,832,256]{3,2,1,0:T(8,128)} custom-call(bf16[832,832]{1,0:T(8,128)(2,1)S(1)} %copy-done.4, bf16[256,256]{1,0:T(8,128)(2,1)S(1)} %copy-done.3, bf16[3328,2048]{1,0:T(8,128)(2,1)} %refs_1_.15, bf16[3328,2048]{1,0:T(8,128)(2,1)} %refs_1_.15, f32[2,208,256]{2,1,0:T(8,128)S(1)} %get-tuple-element.55.refs_2_.refs_4_.refs_0_), custom_call_target="tpu_custom_call" | custom-call | tf_op jit(solution)/shard_map/make_pieces/pallas_call | solution.py:317
  137.8 44.9 %all-to-all-done.1.refs_0_ = f32[8,1,416,256]{3,2,1,0:T(8,128)} async-done(((f32[8,1,416,256]{3,2,1,0:T(8,128)}), f32[8,1,416,256]{3,2,1,0:T(8,128)}, u32[]{:S(2)}, u32[]{:S(2)}) %all-to-all-start.1) | async-done | bytes 3407904 | tf_op jit(solution)/shard_map/all_to_all | solution.py:179
  205.2 22.1 %make_pieces.12.refs_9_ = f32[8,1,832,256]{3,2,1,0:T(8,128)} custom-call(bf16[832,832]{1,0:T(8,128)(2,1)S(1)} %copy-done.5, bf16[256,256]{1,0:T(8,128)(2,1)S(1)} %copy-done.3, bf16[3328,2048]{1,0:T(8,128)(2,1)} %refs_1_.15, bf16[3328,2048]{1,0:T(8,128)(2,1)} %refs_1_.15, f32[2,416,256]{2,1,0:T(8,128)S(1)} %get-tuple-element.61.refs_2_.refs_4_.refs_0_), custom_call_target="tpu_custom_call" | custom-call | tf_op jit(solution)/shard_map/make_pieces/pallas_call | solution.py:317
  227.3 108.3 %all-to-all-done.4.refs_0_ = f32[8,1,832,256]{3,2,1,0:T(8,128)} async-done(((f32[8,1,832,256]{3,2,1,0:T(8,128)}), f32[8,1,832,256]{3,2,1,0:T(8,128)}, u32[]{:S(2)}, u32[]{:S(2)}) %all-to-all-start.4) | async-done | bytes 6815776 | tf_op jit(solution)/shard_map/all_to_all | solution.py:179
  335.6 5.6 all-to-all-start.3
  350.3 7.6 %mix_pieces.11 = (f32[2,832,256]{2,1,0:T(8,128)S(1)}, f32[2,832,256]{2,1,0:T(8,128)}, f32[2,832,256]{2,1,0:T(8,128)}, f32[2,832,256]{2,1,0:T(8,128)}) custom-call(f32[8,1,832,256]{3,2,1,0:T(8,128)} %all-to-all-done.4.refs_0_, f32[2,3,8]{2,1,0:T(4,128)S(1)} %reshape.33.refs_1_), custom_call_target="tpu_custom_call" | custom-call | tf_op jit(solution)/shard_map/mix_pieces/pallas_call | solution.py:371
  361.5 13.8 %make_pieces.13.refs_9_ = f32[8,1,416,256]{3,2,1,0:T(8,128)} custom-call(bf16[416,416]{1,0:T(8,128)(2,1)S(1)} %copy-done.11, bf16[256,256]{1,0:T(8,128)(2,1)S(1)} %copy-done.3, bf16[3328,2048]{1,0:T(8,128)(2,1)} %refs_1_.15, bf16[3328,2048]{1,0:T(8,128)(2,1)} %refs_1_.15, f32[2,832,256]{2,1,0:T(8,128)S(1)} %get-tuple-element.67.refs_2_.refs_4_), custom_call_target="tpu_custom_call" | custom-call | tf_op jit(solution)/shard_map/make_pieces/pallas_call | solution.py:317
  375.3 113.6 %all-to-all-done.3.refs_0_ = f32[8,1,832,256]{3,2,1,0:T(8,128)} async-done(((f32[8,1,832,256]{3,2,1,0:T(8,128)}), f32[8,1,832,256]{3,2,1,0:T(8,128)}, u32[]{:S(2)}, u32[]{:S(2)}) %all-to-all-start.3) | async-done | bytes 6815776 | tf_op jit(solution)/shard_map/all_to_all | solution.py:179
  488.9 5.7 all-to-all-start.6
  494.6 7.7 %finish.11 = (bf16[6656,1024]{1,0:T(8,128)(2,1)}, f32[14,8]{1,0:T(8,128)S(1)}) custom-call(f32[2,416,256]{2,1,0:T(8,128)S(1)} %get-tuple-element.61.refs_2_.refs_4_.refs_0_, f32[2,416,256]{2,1,0:T(8,128)S(1)} %copy-done.19, f32[2,416,256]{2,1,0:T(8,128)} %collective-permute-done.7.refs_6_.refs_2_, ...), custom_call_target="tpu_custom_call", output_to_operand_aliasing={{0}: (8, {})} | custom-call | flops 999999995904 | bytes 4000000000 | tf_op jit(solution)/shard_map/finish/pallas_call | solution.py:470
  502.6 7.5 %mix_pieces.12 = (f32[2,832,256]{2,1,0:T(8,128)S(1)}, f32[2,832,256]{2,1,0:T(8,128)}, f32[2,832,256]{2,1,0:T(8,128)}, f32[2,832,256]{2,1,0:T(8,128)}) custom-call(f32[8,1,832,256]{3,2,1,0:T(8,128)} %all-to-all-done.3.refs_0_, f32[2,7,8]{2,1,0:T(8,128)S(1)} %copy.39.refs_1_), custom_call_target="tpu_custom_call" | custom-call | tf_op jit(solution)/shard_map/mix_pieces/pallas_call | solution.py:371
  513.6 11.3 %make_pieces.14.refs_5_ = f32[8,1,208,256]{3,2,1,0:T(8,128)} custom-call(bf16[208,208]{1,0:T(8,128)(2,1)S(1)} %copy-done.8, bf16[256,256]{1,0:T(8,128)(2,1)S(1)} %copy-done.3, bf16[3328,2048]{1,0:T(8,128)(2,1)} %refs_1_.15, bf16[3328,2048]{1,0:T(8,128)(2,1)} %refs_1_.15, f32[2,832,256]{2,1,0:T(8,128)S(1)} %get-tuple-element.73.refs_2_.refs_0_), custom_call_target="tpu_custom_call" | custom-call | tf_op jit(solution)/shard_map/make_pieces/pallas_call | solution.py:317
  525.0 44.7 %all-to-all-done.6.refs_0_ = f32[8,1,416,256]{3,2,1,0:T(8,128)} async-done(((f32[8,1,416,256]{3,2,1,0:T(8,128)}), f32[8,1,416,256]{3,2,1,0:T(8,128)}, u32[]{:S(2)}, u32[]{:S(2)}) %all-to-all-start.6) | async-done | bytes 3407904 | tf_op jit(solution)/shard_map/all_to_all | solution.py:179
  574.8 13.2 %collective-permute-done.14.refs_3_ = f32[2,832,256]{2,1,0:T(8,128)} collective-permute-done((f32[2,832,256]{2,1,0:T(8,128)}, f32[2,832,256]{2,1,0:T(8,128)}, u32[]{:S(2)}, u32[]{:S(2)}) %collective-permute-start.14) | collective-permute-done | bytes 1703968 | tf_op jit(solution)/shard_map/ppermute | solution.py:198
  588.0 6.1 finish.12
  601.7 11.3 %make_pieces.15.refs_9_ = f32[8,1,208,256]{3,2,1,0:T(8,128)} custom-call(bf16[208,208]{1,0:T(8,128)(2,1)S(1)} %copy-done.9, bf16[256,256]{1,0:T(8,128)(2,1)S(1)} %copy-done.3, bf16[3328,2048]{1,0:T(8,128)(2,1)} %refs_1_.15, bf16[3328,2048]{1,0:T(8,128)(2,1)} %refs_1_.15, f32[2,416,256]{2,1,0:T(8,128)S(1)} %get-tuple-element.79.refs_2_.refs_4_.refs_0_), custom_call_target="tpu_custom_call" | custom-call | tf_op jit(solution)/shard_map/make_pieces/pallas_call | solution.py:317
  619.8 19.2 %collective-permute-done.17.refs_7_.refs_3_ = f32[2,416,256]{2,1,0:T(8,128)} collective-permute-done((f32[2,416,256]{2,1,0:T(8,128)}, f32[2,416,256]{2,1,0:T(8,128)}, u32[]{:S(2)}, u32[]{:S(2)}) %collective-permute-start.17) | collective-permute-done | bytes 852000 | tf_op jit(solution)/shard_map/ppermute | solution.py:198
  676.5 9.8 %collective-permute-done.23.refs_7_ = f32[2,208,256]{2,1,0:T(8,128)} collective-permute-done((f32[2,208,256]{2,1,0:T(8,128)}, f32[2,208,256]{2,1,0:T(8,128)}, u32[]{:S(2)}, u32[]{:S(2)}) %collective-permute-start.23) | collective-permute-done | bytes 426016 | tf_op jit(solution)/shard_map/ppermute | solution.py:198
  (158 shorter events, 125.2 us)
Async XLA Ops:
  13.8 45.5 %all-to-all-start = ((f32[8,1,208,256]{3,2,1,0:T(8,128)}), f32[8,1,208,256]{3,2,1,0:T(8,128)S(1)}, u32[]{:S(2)}, u32[]{:S(2)}) async-start(f32[8,1,208,256]{3,2,1,0:T(8,128)} %make_pieces.8.refs_2_), calls=%async_computation | async-start | bytes 3407872 | tf_op jit(solution)/shard_map/all_to_all | solution.py:179
  59.2 43.8 %all-to-all-start.2 = ((f32[8,1,208,256]{3,2,1,0:T(8,128)}), f32[8,1,208,256]{3,2,1,0:T(8,128)S(1)}, u32[]{:S(2)}, u32[]{:S(2)}) async-start(f32[8,1,208,256]{3,2,1,0:T(8,128)} %make_pieces.9.refs_1_), calls=%async_computation.2 | async-start | bytes 3407872 | tf_op jit(solution)/shard_map/all_to_all | solution.py:179
  65.9 41.8 %collective-permute-start = (f32[2,208,256]{2,1,0:T(8,128)}, f32[2,208,256]{2,1,0:T(8,128)S(1)}, u32[]{:S(2)}, u32[]{:S(2)}) collective-permute-start(f32[2,208,256]{2,1,0:T(8,128)} %get-tuple-element.51), channel_id=1, source_target_pairs={{0,1},{1,0},{2,3},{3,2},{4,5},{5,4},{6,7},{7,6},{8,9},{9,8},{10,11... | collective-permute-start | bytes 1277960 | tf_op jit(solution)/shard_map/ppermute | solution.py:198
  66.7 41.0 %collective-permute-start.1 = (f32[2,208,256]{2,1,0:T(8,128)}, f32[2,208,256]{2,1,0:T(8,128)S(1)}, u32[]{:S(2)}, u32[]{:S(2)}) collective-permute-start(f32[2,208,256]{2,1,0:T(8,128)} %get-tuple-element.52), channel_id=1, source_target_pairs={{0,2},{1,3},{2,0},{3,1},{4,6},{5,7},{6,4},{7,5},{8,10},{9,11},{10,... | collective-permute-start | bytes 1277960 | tf_op jit(solution)/shard_map/ppermute | solution.py:198
  67.9 39.8 %collective-permute-start.2 = (f32[2,208,256]{2,1,0:T(8,128)}, f32[2,208,256]{2,1,0:T(8,128)S(1)}, u32[]{:S(2)}, u32[]{:S(2)}) collective-permute-start(f32[2,208,256]{2,1,0:T(8,128)} %get-tuple-element.53), channel_id=1, source_target_pairs={{0,3},{1,2},{2,1},{3,0},{4,7},{5,6},{6,5},{7,4},{8,11},{9,10},{10,... | collective-permute-start | bytes 1277960 | tf_op jit(solution)/shard_map/ppermute | solution.py:198
  103.1 79.6 %all-to-all-start.1 = ((f32[8,1,416,256]{3,2,1,0:T(8,128)}), f32[8,1,416,256]{3,2,1,0:T(8,128)}, u32[]{:S(2)}, u32[]{:S(2)}) async-start(f32[8,1,416,256]{3,2,1,0:T(8,128)} %make_pieces.10.refs_4_), calls=%async_computation.1 | async-start | bytes 6815744 | tf_op jit(solution)/shard_map/all_to_all | solution.py:179
  112.5 75.5 %collective-permute-start.3 = (f32[2,208,256]{2,1,0:T(8,128)}, f32[2,208,256]{2,1,0:T(8,128)S(1)}, u32[]{:S(2)}, u32[]{:S(2)}) collective-permute-start(f32[2,208,256]{2,1,0:T(8,128)} %get-tuple-element.56), channel_id=1, source_target_pairs={{0,1},{1,0},{2,3},{3,2},{4,5},{5,4},{6,7},{7,6},{8,9},{9,8},{10,11... | collective-permute-start | bytes 1277960 | tf_op jit(solution)/shard_map/ppermute | solution.py:198
  114.1 73.9 %collective-permute-start.4 = (f32[2,208,256]{2,1,0:T(8,128)}, f32[2,208,256]{2,1,0:T(8,128)S(1)}, u32[]{:S(2)}, u32[]{:S(2)}) collective-permute-start(f32[2,208,256]{2,1,0:T(8,128)} %get-tuple-element.57), channel_id=1, source_target_pairs={{0,2},{1,3},{2,0},{3,1},{4,6},{5,7},{6,4},{7,5},{8,10},{9,11},{10,... | collective-permute-start | bytes 1277960 | tf_op jit(solution)/shard_map/ppermute | solution.py:198
  115.3 72.7 %collective-permute-start.5 = (f32[2,208,256]{2,1,0:T(8,128)}, f32[2,208,256]{2,1,0:T(8,128)S(1)}, u32[]{:S(2)}, u32[]{:S(2)}) collective-permute-start(f32[2,208,256]{2,1,0:T(8,128)} %get-tuple-element.58), channel_id=1, source_target_pairs={{0,3},{1,2},{2,1},{3,0},{4,7},{5,6},{6,5},{7,4},{8,11},{9,10},{10,... | collective-permute-start | bytes 1277960 | tf_op jit(solution)/shard_map/ppermute | solution.py:198
  182.7 152.9 %all-to-all-start.4 = ((f32[8,1,832,256]{3,2,1,0:T(8,128)}), f32[8,1,832,256]{3,2,1,0:T(8,128)}, u32[]{:S(2)}, u32[]{:S(2)}) async-start(f32[8,1,832,256]{3,2,1,0:T(8,128)} %make_pieces.11.refs_9_), calls=%async_computation.4 | async-start | bytes 13631488 | tf_op jit(solution)/shard_map/all_to_all | solution.py:179
  201.4 139.8 %collective-permute-start.6 = (f32[2,416,256]{2,1,0:T(8,128)}, f32[2,416,256]{2,1,0:T(8,128)S(1)}, u32[]{:S(2)}, u32[]{:S(2)}) collective-permute-start(f32[2,416,256]{2,1,0:T(8,128)} %get-tuple-element.62), channel_id=1, source_target_pairs={{0,1},{1,0},{2,3},{3,2},{4,5},{5,4},{6,7},{7,6},{8,9},{9,8},{10,11... | collective-permute-start | bytes 2555912 | tf_op jit(solution)/shard_map/ppermute | solution.py:198
  203.4 137.8 %collective-permute-start.7 = (f32[2,416,256]{2,1,0:T(8,128)}, f32[2,416,256]{2,1,0:T(8,128)}, u32[]{:S(2)}, u32[]{:S(2)}) collective-permute-start(f32[2,416,256]{2,1,0:T(8,128)} %get-tuple-element.63), channel_id=1, source_target_pairs={{0,2},{1,3},{2,0},{3,1},{4,6},{5,7},{6,4},{7,5},{8,10},{9,11},{10,... | collective-permute-start | bytes 2555912 | tf_op jit(solution)/shard_map/ppermute | solution.py:198
  204.7 136.6 %collective-permute-start.8 = (f32[2,416,256]{2,1,0:T(8,128)}, f32[2,416,256]{2,1,0:T(8,128)}, u32[]{:S(2)}, u32[]{:S(2)}) collective-permute-start(f32[2,416,256]{2,1,0:T(8,128)} %get-tuple-element.64), channel_id=1, source_target_pairs={{0,3},{1,2},{2,1},{3,0},{4,7},{5,6},{6,5},{7,4},{8,11},{9,10},{10,... | collective-permute-start | bytes 2555912 | tf_op jit(solution)/shard_map/ppermute | solution.py:198
  335.6 153.3 %all-to-all-start.3 = ((f32[8,1,832,256]{3,2,1,0:T(8,128)}), f32[8,1,832,256]{3,2,1,0:T(8,128)}, u32[]{:S(2)}, u32[]{:S(2)}) async-start(f32[8,1,832,256]{3,2,1,0:T(8,128)} %make_pieces.12.refs_9_), calls=%async_computation.3 | async-start | bytes 13631488 | tf_op jit(solution)/shard_map/all_to_all | solution.py:179
  357.9 136.7 %collective-permute-start.10 = (f32[2,832,256]{2,1,0:T(8,128)}, f32[2,832,256]{2,1,0:T(8,128)}, u32[]{:S(2)}, u32[]{:S(2)}) collective-permute-start(f32[2,832,256]{2,1,0:T(8,128)} %get-tuple-element.69), channel_id=1, source_target_pairs={{0,2},{1,3},{2,0},{3,1},{4,6},{5,7},{6,4},{7,5},{8,10},{9,11},{10,... | collective-permute-start | bytes 5111816 | tf_op jit(solution)/shard_map/ppermute | solution.py:198
  359.1 135.5 %collective-permute-start.11 = (f32[2,832,256]{2,1,0:T(8,128)}, f32[2,832,256]{2,1,0:T(8,128)}, u32[]{:S(2)}, u32[]{:S(2)}) collective-permute-start(f32[2,832,256]{2,1,0:T(8,128)} %get-tuple-element.70), channel_id=1, source_target_pairs={{0,3},{1,2},{2,1},{3,0},{4,7},{5,6},{6,5},{7,4},{8,11},{9,10},{10,... | collective-permute-start | bytes 5111816 | tf_op jit(solution)/shard_map/ppermute | solution.py:198
  361.5 133.1 %collective-permute-start.9 = (f32[2,832,256]{2,1,0:T(8,128)}, f32[2,832,256]{2,1,0:T(8,128)}, u32[]{:S(2)}, u32[]{:S(2)}) collective-permute-start(f32[2,832,256]{2,1,0:T(8,128)} %get-tuple-element.68), channel_id=1, source_target_pairs={{0,1},{1,0},{2,3},{3,2},{4,5},{5,4},{6,7},{7,6},{8,9},{9,8},{10,11... | collective-permute-start | bytes 5111816 | tf_op jit(solution)/shard_map/ppermute | solution.py:198
  488.9 80.8 %all-to-all-start.6 = ((f32[8,1,416,256]{3,2,1,0:T(8,128)}), f32[8,1,416,256]{3,2,1,0:T(8,128)}, u32[]{:S(2)}, u32[]{:S(2)}) async-start(f32[8,1,416,256]{3,2,1,0:T(8,128)} %make_pieces.13.refs_9_), calls=%async_computation.6 | async-start | bytes 6815744 | tf_op jit(solution)/shard_map/all_to_all | solution.py:179
  510.1 64.7 %collective-permute-start.12 = (f32[2,832,256]{2,1,0:T(8,128)}, f32[2,832,256]{2,1,0:T(8,128)}, u32[]{:S(2)}, u32[]{:S(2)}) collective-permute-start(f32[2,832,256]{2,1,0:T(8,128)} %get-tuple-element.74), channel_id=1, source_target_pairs={{0,1},{1,0},{2,3},{3,2},{4,5},{5,4},{6,7},{7,6},{8,9},{9,8},{10,11... | collective-permute-start | bytes 5111816 | tf_op jit(solution)/shard_map/ppermute | solution.py:198
  511.9 62.9 %collective-permute-start.13 = (f32[2,832,256]{2,1,0:T(8,128)}, f32[2,832,256]{2,1,0:T(8,128)}, u32[]{:S(2)}, u32[]{:S(2)}) collective-permute-start(f32[2,832,256]{2,1,0:T(8,128)} %get-tuple-element.75), channel_id=1, source_target_pairs={{0,2},{1,3},{2,0},{3,1},{4,6},{5,7},{6,4},{7,5},{8,10},{9,11},{10,... | collective-permute-start | bytes 5111816 | tf_op jit(solution)/shard_map/ppermute | solution.py:198
  513.1 74.8 %collective-permute-start.14 = (f32[2,832,256]{2,1,0:T(8,128)}, f32[2,832,256]{2,1,0:T(8,128)}, u32[]{:S(2)}, u32[]{:S(2)}) collective-permute-start(f32[2,832,256]{2,1,0:T(8,128)} %get-tuple-element.76), channel_id=1, source_target_pairs={{0,3},{1,2},{2,1},{3,0},{4,7},{5,6},{6,5},{7,4},{8,11},{9,10},{10,... | collective-permute-start | bytes 5111816 | tf_op jit(solution)/shard_map/ppermute | solution.py:198
  569.7 43.7 %all-to-all-start.5 = ((f32[8,1,208,256]{3,2,1,0:T(8,128)}), f32[8,1,208,256]{3,2,1,0:T(8,128)}, u32[]{:S(2)}, u32[]{:S(2)}) async-start(f32[8,1,208,256]{3,2,1,0:T(8,128)} %make_pieces.14.refs_5_), calls=%async_computation.5 | async-start | bytes 3407872 | tf_op jit(solution)/shard_map/all_to_all | solution.py:179
  600.7 38.3 %collective-permute-start.17 = (f32[2,416,256]{2,1,0:T(8,128)}, f32[2,416,256]{2,1,0:T(8,128)}, u32[]{:S(2)}, u32[]{:S(2)}) collective-permute-start(f32[2,416,256]{2,1,0:T(8,128)} %get-tuple-element.82), channel_id=1, source_target_pairs={{0,3},{1,2},{2,1},{3,0},{4,7},{5,6},{6,5},{7,4},{8,11},{9,10},{10,... | collective-permute-start | bytes 2555912 | tf_op jit(solution)/shard_map/ppermute | solution.py:198
  613.4 43.8 %all-to-all-start.7 = ((f32[8,1,208,256]{3,2,1,0:T(8,128)}), f32[8,1,208,256]{3,2,1,0:T(8,128)}, u32[]{:S(2)}, u32[]{:S(2)}) async-start(f32[8,1,208,256]{3,2,1,0:T(8,128)} %make_pieces.15.refs_9_), calls=%async_computation.7 | async-start | bytes 3407872 | tf_op jit(solution)/shard_map/all_to_all | solution.py:179
  (47 other events, 529.8 us)

commit v3 on v2

--- a/solution.py
+++ b/solution.py
@@ -225,10 +225,10 @@
             return [jax.ShapeDtypeStruct((self.fan, slots, rows, piece), jnp.float32)]
         return [jax.ShapeDtypeStruct((slots, rows, piece), jnp.float32)] * self.fan
 
-    def blocks(self, slots, rows, piece, moving, arrived=False):
-        where = (lambda step: (0, step, 0)) if moving else (lambda step: (0, 0, 0))
+    def blocks(self, slots, rows, piece, arrived=False):
+        where = lambda at, *inner: (0, at, 0)
         if self.kind != "xor":
-            whole = pl.BlockSpec((self.fan, slots, rows, piece), lambda step: (0,) + where(step))
+            whole = pl.BlockSpec((self.fan, slots, rows, piece), lambda *at: (0,) + where(*at))
             after = [pl.BlockSpec((slots, rows, piece), where)] if self.kind == "sum" and arrived else []
             return [whole] + after
         return [pl.BlockSpec((slots, rows, piece), where)] * self.fan
@@ -251,15 +251,13 @@
     return sums
 
 
-def make_pieces(weight, first, count, parts, after, stage, labels):
+def make_pieces(weight, first, count, at_once, parts, after, stage, labels):
     rows_dev, cols_dev = weight.shape
     piece = cols_dev // parts
     sub_rows = rows_dev // PALEY
-    rows = count * PALEY
-    order = sylvester(sub_rows)
-    base = jnp.asarray(np.kron(order[:count, :count], paley_signs()), jnp.bfloat16)
+    rows = at_once * PALEY
+    base = jnp.asarray(np.kron(sylvester(at_once), paley_signs()), jnp.bfloat16)
     inner = jnp.asarray(sylvester(piece), jnp.bfloat16)
-    far_signs = order[first, ::count]
     names = labels.start()
     cut = [labels.split(*bit) for bit in stage.bits]
     rest_names = [name for name in names if name not in cut]
@@ -271,7 +269,11 @@
     def kernel(base_ref, inner_ref, *refs):
         w_refs, refs = refs[:SPLIT], refs[SPLIT:]
         outs, held, summed = refs[len(after):-2], refs[-2], refs[-1]
-        step = pl.program_id(0)
+        turn, step = pl.program_id(0), pl.program_id(1)
+        far_signs = [
+            parity_sign((first + turn * at_once) & far, sub_rows)
+            for far in range(0, sub_rows, at_once)
+        ]
         me = None if stage.kind == "all" else lax.axis_index("fsdp")
 
         def gather(at, carry):
@@ -280,7 +282,7 @@
             for far, sign in enumerate(far_signs):
                 part, inside = divmod(far * rows, rows_dev // SPLIT)
                 term = w_refs[part][pl.ds(here + inside, 16), :].astype(jnp.float32)
-                total = term if total is None else total + term if sign > 0 else total - term
+                total = term if total is None else total + sign * term
             summed[pl.ds(here, 16), :] = total
             return carry
 
@@ -312,22 +314,22 @@
 
             lax.fori_loop(0, rows // 8, body, 0)
 
-    whole = lambda step: (0, 0)
+    whole = lambda turn, step: (0, 0)
     slots = 1 << len(rest_names)
     return pl.pallas_call(
         kernel,
-        grid=(parts,),
+        grid=(count // at_once, parts),
         in_specs=[
             pl.BlockSpec((rows, rows), whole, pipeline_mode=pl.Buffered(1)),
             pl.BlockSpec((piece, piece), whole, pipeline_mode=pl.Buffered(1)),
         ]
         + [
-            pl.BlockSpec((rows_dev // SPLIT, piece), functools.partial(lambda part, step: (part, step), part))
+            pl.BlockSpec((rows_dev // SPLIT, piece), functools.partial(lambda part, turn, step: (part, step), part))
             for part in range(SPLIT)
         ]
         + [ANYWHERE] * len(after),
-        out_specs=stage.blocks(slots, rows, piece, False),
-        out_shape=stage.shapes(slots, rows, piece),
+        out_specs=stage.blocks(slots, rows, piece),
+        out_shape=stage.shapes(slots, count * PALEY, piece),
         scratch_shapes=[
             pltpu.VMEM((parts, rows, piece), jnp.float32),
             pltpu.VMEM((rows, piece), jnp.float32),
@@ -371,8 +373,8 @@
     return pl.pallas_call(
         kernel,
         grid=(rows // tile,),
-        in_specs=came.blocks(slots_in, tile, piece, True, True) + [ANYWHERE] * len(after),
-        out_specs=going.blocks(slots_out, tile, piece, True),
+        in_specs=came.blocks(slots_in, tile, piece, True) + [ANYWHERE] * len(after),
+        out_specs=going.blocks(slots_out, tile, piece),
         out_shape=going.shapes(slots_out, rows, piece),
         compiler_params=compiler_params(24 * 2**20),
         cost_estimate=TINY,
@@ -494,13 +496,14 @@
     grp = [("grp", i) for i in range(labels.groups_bits)]
     unit = sub_rows // 16
     stages = [Stage("all", every), Stage("xor", grp)]
-    chunks = [(unit * times, stages) for times in (1, 1, 2, 4, 4, 2, 1, 1)]
+    spans = ((14, 1, 1), (0, 8, 4), (8, 4, 4), (12, 2, 2), (15, 1, 1))
+    chunks = [(unit * first, unit * count, unit * at_once, stages) for first, count, at_once in spans]
     n = len(chunks)
     order = [0, 1]
     for c in range(n):
+        order += [c]
         if c >= 1 and c < n - 1:
             order += [c - 1]
-        order += [c]
         if c + 2 < n:
             order += [c + 2]
     return chunks, order + [n - 2, n - 1]
@@ -513,14 +516,13 @@
     sub_rows = rows_dev // PALEY
     labels = Labels(parts, groups)
     chunks, order = plan(sub_rows, labels)
-    firsts = np.cumsum([0] + [count for count, _ in chunks])
     state = {}
     result, scales, finished, token = None, [], [], ()
     for c in order:
-        count, stages = chunks[c]
+        first, count, at_once, stages = chunks[c]
         if c not in state:
             arrays, names = make_pieces(
-                weight, int(firsts[c]), count, parts, token, stages[0], labels
+                weight, first, count, at_once, parts, token, stages[0], labels
             )
             token = (arrays[0],)
             state[c] = (0, stages[0].send(arrays), names)
@@ -532,7 +534,7 @@
             token = (arrays[0],)
             state[c] = (at + 1, stages[at + 1].send(arrays), names)
             continue
-        low, high = int(firsts[c]) * PALEY, int(firsts[c + 1]) * PALEY
+        low, high = first * PALEY, (first + count) * PALEY
         finished.append((low, high, arrays, names, stages[at]))
         ready = [
             b

time: 694 us -> 674 us (0.971)
  Pallas kernels: 190 us -> 162 us
  waiting for transfers between devices: 416 us -> 443 us
  starting transfers between devices: 67.3 us -> 45.2 us
    all_to_all x8 -> x5, waiting for transfers between devices: 365 us -> 430 us  [send(): lax.all_to_all(arrays[0], self.bits[0][0], split_axis=0, concat_axis=0, t...]
    ppermute x24 -> x15, waiting for transfers between devices: 50.7 us -> 13.3 us  [send(): received.append(lax.ppermute(arrays[e], axis, pairs))]
    pallas_call x8 -> x5, Pallas kernels: 117 us -> 102 us  [make_pieces(): pl.pallas_call(kernel, grid=(count // at_once, parts), in_specs=[pl.Block...]
    all_to_all x8 -> x5, starting transfers between devices: 42.6 us -> 28.1 us  [send(): lax.all_to_all(arrays[0], self.bits[0][0], split_axis=0, concat_axis=0, t...]
    pallas_call x8 -> x5, Pallas kernels: 37.9 us -> 29.5 us  [finish(): pl.pallas_call(kernel, in_specs=[ANYWHERE] * (len(operands) + int(aliased...]
    ppermute x24 -> x15, starting transfers between devices: 24.6 us -> 17.2 us  [send(): received.append(lax.ppermute(arrays[e], axis, pairs))]
    unnamed x78 -> x58, local copies, waits for them, and re-layouts: 12.6 us -> 17.5 us
    pallas_call x8 -> x5, Pallas kernels: 35.2 us -> 31.1 us  [mix_pieces(): pl.pallas_call(kernel, grid=(rows // tile,), in_specs=came.blocks(slots_i...]
  transfers between devices with their start and end apart: 32 -> 20, of which waited for: 14 -> 6; matrix products, arithmetic and copies ran while one was open for 1% -> 0% of each run, Pallas kernels for 25% -> 22%
where the time goes in v3:
time: 674 us; the launch traced here: 672 us
  waiting for transfers between devices  443 us (66%)
  Pallas kernels  162 us (24%)
  starting transfers between devices  45.2 us (7%)
  local copies, waits for them, and re-layouts  20.2 us (3%)
    all_to_all x5, waiting for transfers between devices, send(): lax.all_to_all(arrays[0], self.bits[0][0], split_axis=0, concat_axis=0, t...  430 us
    pallas_call x5, Pallas kernels, make_pieces(): pl.pallas_call(kernel, grid=(count // at_once, parts), in_specs=[pl.Block...  102 us
    pallas_call x5, Pallas kernels, mix_pieces(): pl.pallas_call(kernel, grid=(rows // tile,), in_specs=came.blocks(slots_i...  31.1 us
    pallas_call x5, Pallas kernels, finish(): pl.pallas_call(kernel, in_specs=[ANYWHERE] * (len(operands) + int(aliased...  29.5 us
    all_to_all x5, starting transfers between devices, send(): lax.all_to_all(arrays[0], self.bits[0][0], split_axis=0, concat_axis=0, t...  28.1 us
    unnamed x58, local copies, waits for them, and re-layouts  17.5 us
    ppermute x15, starting transfers between devices, send(): received.append(lax.ppermute(arrays[e], axis, pairs))  17.2 us
  transfers between devices with their start and end apart: 20, of which 6 were waited for; matrix products, arithmetic and copies ran while one was open for 0% of the time, Pallas kernels for 22%

profile of v3, /device:TPU:1, one launch (start us, length us, event | category | flops | bytes accessed | tf_op | source)
XLA Modules:
  0.0 672.2 jit_solution(1522969927200027868)
XLA Ops:
  2.4 11.6 %make_pieces.5.refs_2_ = f32[8,1,208,256]{3,2,1,0:T(8,128)} custom-call(bf16[208,208]{1,0:T(8,128)(2,1)S(1)} %copy-done.5, bf16[256,256]{1,0:T(8,128)(2,1)S(1)} %copy-done.3, bf16[3328,2048]{1,0:T(8,128)(2,1)} %refs_1_.9, bf16[3328,2048]{1,0:T(8,128)(2,1)} %refs_1_.9), custom_call_target="tpu_custom_call" | custom-call | tf_op jit(solution)/shard_map/make_pieces/pallas_call | solution.py:319
  14.1 6.5 all-to-all-start
  20.6 42.2 %make_pieces.6.refs_1_ = f32[8,1,1664,256]{3,2,1,0:T(8,128)} custom-call(bf16[832,832]{1,0:T(8,128)(2,1)S(1)} %copy-done.2, bf16[256,256]{1,0:T(8,128)(2,1)S(1)} %copy-done.4, bf16[3328,2048]{1,0:T(8,128)(2,1)} %refs_1_.9, bf16[3328,2048]{1,0:T(8,128)(2,1)} %refs_1_.9, f32[8,1,208,256]{3,2,1,0:T(8,128)} %make_pieces.5.refs_2_), custom_call_target="tpu_custom_call" | custom-call | tf_op jit(solution)/shard_map/make_pieces/pallas_call | solution.py:319
  62.8 5.5 all-to-all-start.1
  68.3 4.9 copy-done
  78.3 22.2 %make_pieces.7.refs_1_ = f32[8,1,832,256]{3,2,1,0:T(8,128)} custom-call(bf16[832,832]{1,0:T(8,128)(2,1)S(1)} %copy-done.2, bf16[256,256]{1,0:T(8,128)(2,1)S(1)} %copy-done.4, bf16[3328,2048]{1,0:T(8,128)(2,1)} %refs_1_.9, bf16[3328,2048]{1,0:T(8,128)(2,1)} %refs_1_.9, f32[2,208,256]{2,1,0:T(8,128)S(1)} %get-tuple-element.32.refs_2_.refs_0_), custom_call_target="tpu_custom_call" | custom-call | tf_op jit(solution)/shard_map/make_pieces/pallas_call | solution.py:319
  101.3 261.0 %all-to-all-done.1.refs_0_ = f32[8,1,1664,256]{3,2,1,0:T(8,128)} async-done(((f32[8,1,1664,256]{3,2,1,0:T(8,128)}), f32[8,1,1664,256]{3,2,1,0:T(8,128)}, u32[]{:S(2)}, u32[]{:S(2)}) %all-to-all-start.1) | async-done | bytes 13631520 | tf_op jit(solution)/shard_map/all_to_all | solution.py:179
  362.3 5.3 all-to-all-start.2
  370.6 13.6 %mix_pieces.6 = (f32[2,1664,256]{2,1,0:T(8,128)S(1)}, f32[2,1664,256]{2,1,0:T(8,128)}, f32[2,1664,256]{2,1,0:T(8,128)}, f32[2,1664,256]{2,1,0:T(8,128)}) custom-call(f32[8,1,1664,256]{3,2,1,0:T(8,128)} %all-to-all-done.1.refs_0_, f32[8,1,832,256]{3,2,1,0:T(8,128)S(1)} %copy-done.1), custom_call_target="tpu_custom_call" | custom-call | tf_op jit(solution)/shard_map/mix_pieces/pallas_call | solution.py:373
  390.5 14.0 %make_pieces.8.refs_1_ = f32[8,1,416,256]{3,2,1,0:T(8,128)} custom-call(bf16[416,416]{1,0:T(8,128)(2,1)S(1)} %copy-done.10, bf16[256,256]{1,0:T(8,128)(2,1)S(1)} %copy-done.4, bf16[3328,2048]{1,0:T(8,128)(2,1)} %refs_1_.9, bf16[3328,2048]{1,0:T(8,128)(2,1)} %refs_1_.9, f32[2,1,8]{2,1,0:T(1,128)S(1)} %bitcast.11), custom_call_target="tpu_custom_call" | custom-call | tf_op jit(solution)/shard_map/make_pieces/pallas_call | solution.py:319
  404.5 110.8 %all-to-all-done.2.refs_0_ = f32[8,1,832,256]{3,2,1,0:T(8,128)} async-done(((f32[8,1,832,256]{3,2,1,0:T(8,128)}), f32[8,1,832,256]{3,2,1,0:T(8,128)}, u32[]{:S(2)}, u32[]{:S(2)}) %all-to-all-start.2) | async-done | bytes 6815776 | tf_op jit(solution)/shard_map/all_to_all | solution.py:179
  515.3 5.5 all-to-all-start.4
  520.8 7.5 %mix_pieces.7 = (f32[2,832,256]{2,1,0:T(8,128)S(1)}, f32[2,832,256]{2,1,0:T(8,128)}, f32[2,832,256]{2,1,0:T(8,128)}, f32[2,832,256]{2,1,0:T(8,128)}) custom-call(f32[8,1,832,256]{3,2,1,0:T(8,128)} %all-to-all-done.2.refs_0_, f32[8,1,416,256]{3,2,1,0:T(8,128)} %make_pieces.8.refs_1_), custom_call_target="tpu_custom_call" | custom-call | tf_op jit(solution)/shard_map/mix_pieces/pallas_call | solution.py:373
  537.5 12.5 %finish.6 = (bf16[6656,1024]{1,0:T(8,128)(2,1)}, f32[26,8]{1,0:T(8,128)S(1)}) custom-call(f32[2,1664,256]{2,1,0:T(8,128)S(1)} %copy-done.12, f32[2,1664,256]{2,1,0:T(8,128)} %collective-permute-done.3.refs_1_, f32[2,1664,256]{2,1,0:T(8,128)} %collective-permute-done.4.refs_2_, ...), custom_call_target="tpu_custom_call", output_to_operand_aliasing={{0}: (4, {})} | custom-call | flops 999999995904 | bytes 4000000000 | tf_op jit(solution)/shard_map/finish/pallas_call | solution.py:472
  550.3 11.6 %make_pieces.9.refs_1_ = f32[8,1,208,256]{3,2,1,0:T(8,128)} custom-call(bf16[208,208]{1,0:T(8,128)(2,1)S(1)} %copy-done.6, bf16[256,256]{1,0:T(8,128)(2,1)S(1)} %copy-done.4, bf16[3328,2048]{1,0:T(8,128)(2,1)} %refs_1_.9, bf16[3328,2048]{1,0:T(8,128)(2,1)} %refs_1_.9, f32[2,13,8]{2,1,0:T(8,128)S(1)} %copy.25.refs_2_), custom_call_target="tpu_custom_call" | custom-call | tf_op jit(solution)/shard_map/make_pieces/pallas_call | solution.py:319
  561.9 33.9 %all-to-all-done.4.refs_0_ = f32[8,1,416,256]{3,2,1,0:T(8,128)} async-done(((f32[8,1,416,256]{3,2,1,0:T(8,128)}), f32[8,1,416,256]{3,2,1,0:T(8,128)}, u32[]{:S(2)}, u32[]{:S(2)}) %all-to-all-start.4) | async-done | bytes 3407904 | tf_op jit(solution)/shard_map/all_to_all | solution.py:179
  595.8 5.3 all-to-all-start.3
  601.1 4.5 mix_pieces.8
  609.0 6.1 finish.7
  615.4 24.5 %all-to-all-done.3.refs_0_ = f32[8,1,208,256]{3,2,1,0:T(8,128)} async-done(((f32[8,1,208,256]{3,2,1,0:T(8,128)}), f32[8,1,208,256]{3,2,1,0:T(8,128)}, u32[]{:S(2)}, u32[]{:S(2)}) %all-to-all-start.3) | async-done | bytes 1703968 | tf_op jit(solution)/shard_map/all_to_all | solution.py:179
  639.8 3.4 mix_pieces.9
  649.2 4.9 finish.8
  654.8 10.0 %collective-permute-done.11.refs_7_ = f32[2,208,256]{2,1,0:T(8,128)} collective-permute-done((f32[2,208,256]{2,1,0:T(8,128)}, f32[2,208,256]{2,1,0:T(8,128)}, u32[]{:S(2)}, u32[]{:S(2)}) %collective-permute-start.11) | collective-permute-done | bytes 426016 | tf_op jit(solution)/shard_map/ppermute | solution.py:198
  667.8 3.4 finish.9
  (100 shorter events, 40.5 us)
Async XLA Ops:
  14.1 48.8 %all-to-all-start = ((f32[8,1,208,256]{3,2,1,0:T(8,128)}), f32[8,1,208,256]{3,2,1,0:T(8,128)S(1)}, u32[]{:S(2)}, u32[]{:S(2)}) async-start(f32[8,1,208,256]{3,2,1,0:T(8,128)} %make_pieces.5.refs_2_), calls=%async_computation | async-start | bytes 3407872 | tf_op jit(solution)/shard_map/all_to_all | solution.py:179
  62.8 299.5 %all-to-all-start.1 = ((f32[8,1,1664,256]{3,2,1,0:T(8,128)}), f32[8,1,1664,256]{3,2,1,0:T(8,128)}, u32[]{:S(2)}, u32[]{:S(2)}) async-start(f32[8,1,1664,256]{3,2,1,0:T(8,128)} %make_pieces.6.refs_1_), calls=%async_computation.1 | async-start | bytes 27262976 | tf_op jit(solution)/shard_map/all_to_all | solution.py:179
  75.2 312.0 %collective-permute-start = (f32[2,208,256]{2,1,0:T(8,128)}, f32[2,208,256]{2,1,0:T(8,128)S(1)}, u32[]{:S(2)}, u32[]{:S(2)}) collective-permute-start(f32[2,208,256]{2,1,0:T(8,128)} %get-tuple-element.33), channel_id=1, source_target_pairs={{0,1},{1,0},{2,3},{3,2},{4,5},{5,4},{6,7},{7,6},{8,9},{9,8},{10,11... | collective-permute-start | bytes 1277960 | tf_op jit(solution)/shard_map/ppermute | solution.py:198
  76.7 311.0 %collective-permute-start.1 = (f32[2,208,256]{2,1,0:T(8,128)}, f32[2,208,256]{2,1,0:T(8,128)S(1)}, u32[]{:S(2)}, u32[]{:S(2)}) collective-permute-start(f32[2,208,256]{2,1,0:T(8,128)} %get-tuple-element.34), channel_id=1, source_target_pairs={{0,2},{1,3},{2,0},{3,1},{4,6},{5,7},{6,4},{7,5},{8,10},{9,11},{10,... | collective-permute-start | bytes 1277960 | tf_op jit(solution)/shard_map/ppermute | solution.py:198
  77.9 309.8 %collective-permute-start.2 = (f32[2,208,256]{2,1,0:T(8,128)}, f32[2,208,256]{2,1,0:T(8,128)S(1)}, u32[]{:S(2)}, u32[]{:S(2)}) collective-permute-start(f32[2,208,256]{2,1,0:T(8,128)} %get-tuple-element.35), channel_id=1, source_target_pairs={{0,3},{1,2},{2,1},{3,0},{4,7},{5,6},{6,5},{7,4},{8,11},{9,10},{10,... | collective-permute-start | bytes 1277960 | tf_op jit(solution)/shard_map/ppermute | solution.py:198
  362.3 153.0 %all-to-all-start.2 = ((f32[8,1,832,256]{3,2,1,0:T(8,128)}), f32[8,1,832,256]{3,2,1,0:T(8,128)}, u32[]{:S(2)}, u32[]{:S(2)}) async-start(f32[8,1,832,256]{3,2,1,0:T(8,128)} %make_pieces.7.refs_1_), calls=%async_computation.2 | async-start | bytes 13631488 | tf_op jit(solution)/shard_map/all_to_all | solution.py:179
  370.6 17.2 %copy-start.8 = (f32[2,208,256]{2,1,0:T(8,128)S(1)}, f32[2,208,256]{2,1,0:T(8,128)}, u32[]{:S(2)}) copy-start(f32[2,208,256]{2,1,0:T(8,128)} %copy-done.7) | copy-start | bytes 1277956
  384.1 147.8 %collective-permute-start.3 = (f32[2,1664,256]{2,1,0:T(8,128)}, f32[2,1664,256]{2,1,0:T(8,128)}, u32[]{:S(2)}, u32[]{:S(2)}) collective-permute-start(f32[2,1664,256]{2,1,0:T(8,128)} %get-tuple-element.37), channel_id=1, source_target_pairs={{0,1},{1,0},{2,3},{3,2},{4,5},{5,4},{6,7},{7,6},{8,9},{9,8},{10,11... | collective-permute-start | bytes 10223624 | tf_op jit(solution)/shard_map/ppermute | solution.py:198
  386.0 146.3 %collective-permute-start.4 = (f32[2,1664,256]{2,1,0:T(8,128)}, f32[2,1664,256]{2,1,0:T(8,128)}, u32[]{:S(2)}, u32[]{:S(2)}) collective-permute-start(f32[2,1664,256]{2,1,0:T(8,128)} %get-tuple-element.38), channel_id=1, source_target_pairs={{0,2},{1,3},{2,0},{3,1},{4,6},{5,7},{6,4},{7,5},{8,10},{9,11},{10,... | collective-permute-start | bytes 10223624 | tf_op jit(solution)/shard_map/ppermute | solution.py:198
  387.3 148.3 %collective-permute-start.5 = (f32[2,1664,256]{2,1,0:T(8,128)}, f32[2,1664,256]{2,1,0:T(8,128)}, u32[]{:S(2)}, u32[]{:S(2)}) collective-permute-start(f32[2,1664,256]{2,1,0:T(8,128)} %get-tuple-element.39), channel_id=1, source_target_pairs={{0,3},{1,2},{2,1},{3,0},{4,7},{5,6},{6,5},{7,4},{8,11},{9,10},{10,... | collective-permute-start | bytes 10223624 | tf_op jit(solution)/shard_map/ppermute | solution.py:198
  515.3 80.5 %all-to-all-start.4 = ((f32[8,1,416,256]{3,2,1,0:T(8,128)}), f32[8,1,416,256]{3,2,1,0:T(8,128)}, u32[]{:S(2)}, u32[]{:S(2)}) async-start(f32[8,1,416,256]{3,2,1,0:T(8,128)} %make_pieces.8.refs_1_), calls=%async_computation.4 | async-start | bytes 6815744 | tf_op jit(solution)/shard_map/all_to_all | solution.py:179
  528.4 80.1 %collective-permute-start.6 = (f32[2,832,256]{2,1,0:T(8,128)}, f32[2,832,256]{2,1,0:T(8,128)}, u32[]{:S(2)}, u32[]{:S(2)}) collective-permute-start(f32[2,832,256]{2,1,0:T(8,128)} %get-tuple-element.44), channel_id=1, source_target_pairs={{0,1},{1,0},{2,3},{3,2},{4,5},{5,4},{6,7},{7,6},{8,9},{9,8},{10,11... | collective-permute-start | bytes 5111816 | tf_op jit(solution)/shard_map/ppermute | solution.py:198
  530.0 78.9 %collective-permute-start.7 = (f32[2,832,256]{2,1,0:T(8,128)}, f32[2,832,256]{2,1,0:T(8,128)}, u32[]{:S(2)}, u32[]{:S(2)}) collective-permute-start(f32[2,832,256]{2,1,0:T(8,128)} %get-tuple-element.45), channel_id=1, source_target_pairs={{0,2},{1,3},{2,0},{3,1},{4,6},{5,7},{6,4},{7,5},{8,10},{9,11},{10,... | collective-permute-start | bytes 5111816 | tf_op jit(solution)/shard_map/ppermute | solution.py:198
  531.9 77.0 %collective-permute-start.8 = (f32[2,832,256]{2,1,0:T(8,128)}, f32[2,832,256]{2,1,0:T(8,128)}, u32[]{:S(2)}, u32[]{:S(2)}) collective-permute-start(f32[2,832,256]{2,1,0:T(8,128)} %get-tuple-element.46), channel_id=1, source_target_pairs={{0,3},{1,2},{2,1},{3,0},{4,7},{5,6},{6,5},{7,4},{8,11},{9,10},{10,... | collective-permute-start | bytes 5111816 | tf_op jit(solution)/shard_map/ppermute | solution.py:198
  595.8 44.0 %all-to-all-start.3 = ((f32[8,1,208,256]{3,2,1,0:T(8,128)}), f32[8,1,208,256]{3,2,1,0:T(8,128)}, u32[]{:S(2)}, u32[]{:S(2)}) async-start(f32[8,1,208,256]{3,2,1,0:T(8,128)} %make_pieces.9.refs_1_), calls=%async_computation.3 | async-start | bytes 3407872 | tf_op jit(solution)/shard_map/all_to_all | solution.py:179
  605.6 41.5 %collective-permute-start.12 = (f32[2,416,256]{2,1,0:T(8,128)}, f32[2,416,256]{2,1,0:T(8,128)}, u32[]{:S(2)}, u32[]{:S(2)}) collective-permute-start(f32[2,416,256]{2,1,0:T(8,128)} %get-tuple-element.54), channel_id=1, source_target_pairs={{0,1},{1,0},{2,3},{3,2},{4,5},{5,4},{6,7},{7,6},{8,9},{9,8},{10,11... | collective-permute-start | bytes 2555912 | tf_op jit(solution)/shard_map/ppermute | solution.py:198
  607.3 39.9 %collective-permute-start.13 = (f32[2,416,256]{2,1,0:T(8,128)}, f32[2,416,256]{2,1,0:T(8,128)}, u32[]{:S(2)}, u32[]{:S(2)}) collective-permute-start(f32[2,416,256]{2,1,0:T(8,128)} %get-tuple-element.55), channel_id=1, source_target_pairs={{0,2},{1,3},{2,0},{3,1},{4,6},{5,7},{6,4},{7,5},{8,10},{9,11},{10,... | collective-permute-start | bytes 2555912 | tf_op jit(solution)/shard_map/ppermute | solution.py:198
  608.5 38.7 %collective-permute-start.14 = (f32[2,416,256]{2,1,0:T(8,128)}, f32[2,416,256]{2,1,0:T(8,128)}, u32[]{:S(2)}, u32[]{:S(2)}) collective-permute-start(f32[2,416,256]{2,1,0:T(8,128)} %get-tuple-element.56), channel_id=1, source_target_pairs={{0,3},{1,2},{2,1},{3,0},{4,7},{5,6},{6,5},{7,4},{8,11},{9,10},{10,... | collective-permute-start | bytes 2555912 | tf_op jit(solution)/shard_map/ppermute | solution.py:198
  608.9 38.2 %copy-start.9 = (f32[2,208,256]{2,1,0:T(8,128)S(1)}, f32[2,208,256]{2,1,0:T(8,128)}, u32[]{:S(2)}) copy-start(f32[2,208,256]{2,1,0:T(8,128)} %copy-done.7) | copy-start | bytes 1277956
  608.9 38.2 %copy-start.14 = (f32[2,208,256]{2,1,0:T(8,128)S(1)}, f32[2,208,256]{2,1,0:T(8,128)}, u32[]{:S(2)}) copy-start(f32[2,208,256]{2,1,0:T(8,128)} %copy-done.13) | copy-start | bytes 1277956
  615.3 38.8 %copy-start.25 = (f32[2,6,8]{1,0,2:T(2,128)}, f32[2,6,8]{1,0,2:T(2,128)S(1)}, u32[]{:S(2)}) copy-start(f32[2,6,8]{1,0,2:T(2,128)S(1)} %reshape.24) | copy-start | bytes 1156
  643.3 11.5 %collective-permute-start.10 = (f32[2,208,256]{2,1,0:T(8,128)}, f32[2,208,256]{2,1,0:T(8,128)}, u32[]{:S(2)}, u32[]{:S(2)}) collective-permute-start(f32[2,208,256]{2,1,0:T(8,128)} %get-tuple-element.52), channel_id=1, source_target_pairs={{0,2},{1,3},{2,0},{3,1},{4,6},{5,7},{6,4},{7,5},{8,10},{9,11},{10,... | collective-permute-start | bytes 1277960 | tf_op jit(solution)/shard_map/ppermute | solution.py:198
  644.5 20.3 %collective-permute-start.11 = (f32[2,208,256]{2,1,0:T(8,128)}, f32[2,208,256]{2,1,0:T(8,128)}, u32[]{:S(2)}, u32[]{:S(2)}) collective-permute-start(f32[2,208,256]{2,1,0:T(8,128)} %get-tuple-element.53), channel_id=1, source_target_pairs={{0,3},{1,2},{2,1},{3,0},{4,7},{5,6},{6,5},{7,4},{8,11},{9,10},{10,... | collective-permute-start | bytes 1277960 | tf_op jit(solution)/shard_map/ppermute | solution.py:198
  647.2 17.6 %collective-permute-start.9 = (f32[2,208,256]{2,1,0:T(8,128)}, f32[2,208,256]{2,1,0:T(8,128)}, u32[]{:S(2)}, u32[]{:S(2)}) collective-permute-start(f32[2,208,256]{2,1,0:T(8,128)} %get-tuple-element.51), channel_id=1, source_target_pairs={{0,1},{1,0},{2,3},{3,2},{4,5},{5,4},{6,7},{7,6},{8,9},{9,8},{10,11... | collective-permute-start | bytes 1277960 | tf_op jit(solution)/shard_map/ppermute | solution.py:198
  (25 other events, 97.4 us)

commit v4 on v3

--- a/solution.py
+++ b/solution.py
@@ -302,7 +302,7 @@
             before = [1.0 if me is None else parity_sign(a & me, parts) for a in range(parts)]
 
             def body(at, carry):
-                here = pl.ds(pl.multiple_of(at * 8, 8), 8)
+                here = pl.ds(pl.multiple_of(at * 16, 16), 16)
                 values = [held[a, here, :] for a in range(parts)]
                 if me is not None:
                     values = [values[0]] + [before[a] * values[a] for a in range(1, parts)]
@@ -312,7 +312,7 @@
                     targets[slot_of(cut, digits)][...] = value
                 return carry
 
-            lax.fori_loop(0, rows // 8, body, 0)
+            lax.fori_loop(0, rows // 16, body, 0)
 
     whole = lambda turn, step: (0, 0)
     slots = 1 << len(rest_names)
@@ -346,7 +346,7 @@
     cut = [labels.split(*bit) for bit in going.bits]
     rest_names = [name for name in names + made if name not in cut]
     slots_in, slots_out = 1 << len(names), 1 << len(rest_names)
-    strip, tile = 8, rows
+    strip, tile = 16, rows
     for size in (104, 208):
         if rows % size == 0:
             tile = size

time: 674 us -> 672 us (level)
  transfers between devices with their start and end apart: 20 -> 20, of which waited for: 6 -> 6; matrix products, arithmetic and copies ran while one was open for 0% -> 0% of each run, Pallas kernels for 22% -> 21%
where the time goes in v4:
time: 672 us; the launch traced here: 671 us
  waiting for transfers between devices  447 us (67%)
  Pallas kernels  158 us (24%)
  starting transfers between devices  45.2 us (7%)
  local copies, waits for them, and re-layouts  20.2 us (3%)
    all_to_all x5, waiting for transfers between devices, send(): lax.all_to_all(arrays[0], self.bits[0][0], split_axis=0, concat_axis=0, t...  434 us
    pallas_call x5, Pallas kernels, make_pieces(): pl.pallas_call(kernel, grid=(count // at_once, parts), in_specs=[pl.Block...  100 us
    pallas_call x5, Pallas kernels, finish(): pl.pallas_call(kernel, in_specs=[ANYWHERE] * (len(operands) + int(aliased...  29.5 us
    all_to_all x5, starting transfers between devices, send(): lax.all_to_all(arrays[0], self.bits[0][0], split_axis=0, concat_axis=0, t...  28.1 us
    pallas_call x5, Pallas kernels, mix_pieces(): pl.pallas_call(kernel, grid=(rows // tile,), in_specs=came.blocks(slots_i...  27.7 us
    unnamed x58, local copies, waits for them, and re-layouts  17.5 us
    ppermute x15, starting transfers between devices, send(): received.append(lax.ppermute(arrays[e], axis, pairs))  17.2 us
  transfers between devices with their start and end apart: 20, of which 6 were waited for; matrix products, arithmetic and copies ran while one was open for 0% of the time, Pallas kernels for 21%

profile of v4, /device:TPU:1, one launch (start us, length us, event | category | flops | bytes accessed | tf_op | source)
XLA Modules:
  0.0 670.6 jit_solution(6995984300232209010)
XLA Ops:
  2.4 11.5 %make_pieces.5.refs_2_ = f32[8,1,208,256]{3,2,1,0:T(8,128)} custom-call(bf16[208,208]{1,0:T(8,128)(2,1)S(1)} %copy-done.5, bf16[256,256]{1,0:T(8,128)(2,1)S(1)} %copy-done.3, bf16[3328,2048]{1,0:T(8,128)(2,1)} %refs_1_.9, bf16[3328,2048]{1,0:T(8,128)(2,1)} %refs_1_.9), custom_call_target="tpu_custom_call" | custom-call | tf_op jit(solution)/shard_map/make_pieces/pallas_call | solution.py:319
  14.0 6.5 all-to-all-start
  20.5 41.5 %make_pieces.6.refs_1_ = f32[8,1,1664,256]{3,2,1,0:T(8,128)} custom-call(bf16[832,832]{1,0:T(8,128)(2,1)S(1)} %copy-done.2, bf16[256,256]{1,0:T(8,128)(2,1)S(1)} %copy-done.4, bf16[3328,2048]{1,0:T(8,128)(2,1)} %refs_1_.9, bf16[3328,2048]{1,0:T(8,128)(2,1)} %refs_1_.9, f32[8,1,208,256]{3,2,1,0:T(8,128)} %make_pieces.5.refs_2_), custom_call_target="tpu_custom_call" | custom-call | tf_op jit(solution)/shard_map/make_pieces/pallas_call | solution.py:319
  62.0 5.5 all-to-all-start.1
  67.5 4.9 copy-done
  77.1 21.8 %make_pieces.7.refs_1_ = f32[8,1,832,256]{3,2,1,0:T(8,128)} custom-call(bf16[832,832]{1,0:T(8,128)(2,1)S(1)} %copy-done.2, bf16[256,256]{1,0:T(8,128)(2,1)S(1)} %copy-done.4, bf16[3328,2048]{1,0:T(8,128)(2,1)} %refs_1_.9, bf16[3328,2048]{1,0:T(8,128)(2,1)} %refs_1_.9, f32[2,208,256]{2,1,0:T(8,128)S(1)} %get-tuple-element.32.refs_2_.refs_0_), custom_call_target="tpu_custom_call" | custom-call | tf_op jit(solution)/shard_map/make_pieces/pallas_call | solution.py:319
  99.7 261.8 %all-to-all-done.1.refs_0_ = f32[8,1,1664,256]{3,2,1,0:T(8,128)} async-done(((f32[8,1,1664,256]{3,2,1,0:T(8,128)}), f32[8,1,1664,256]{3,2,1,0:T(8,128)}, u32[]{:S(2)}, u32[]{:S(2)}) %all-to-all-start.1) | async-done | bytes 13631520 | tf_op jit(solution)/shard_map/all_to_all | solution.py:179
  361.5 5.3 all-to-all-start.2
  369.8 12.6 %mix_pieces.6 = (f32[2,1664,256]{2,1,0:T(8,128)S(1)}, f32[2,1664,256]{2,1,0:T(8,128)}, f32[2,1664,256]{2,1,0:T(8,128)}, f32[2,1664,256]{2,1,0:T(8,128)}) custom-call(f32[8,1,1664,256]{3,2,1,0:T(8,128)} %all-to-all-done.1.refs_0_, f32[8,1,832,256]{3,2,1,0:T(8,128)S(1)} %copy-done.1), custom_call_target="tpu_custom_call" | custom-call | tf_op jit(solution)/shard_map/mix_pieces/pallas_call | solution.py:373
  388.7 13.9 %make_pieces.8.refs_1_ = f32[8,1,416,256]{3,2,1,0:T(8,128)} custom-call(bf16[416,416]{1,0:T(8,128)(2,1)S(1)} %copy-done.10, bf16[256,256]{1,0:T(8,128)(2,1)S(1)} %copy-done.4, bf16[3328,2048]{1,0:T(8,128)(2,1)} %refs_1_.9, bf16[3328,2048]{1,0:T(8,128)(2,1)} %refs_1_.9, f32[2,1,8]{2,1,0:T(1,128)S(1)} %bitcast.11), custom_call_target="tpu_custom_call" | custom-call | tf_op jit(solution)/shard_map/make_pieces/pallas_call | solution.py:319
  402.6 111.9 %all-to-all-done.2.refs_0_ = f32[8,1,832,256]{3,2,1,0:T(8,128)} async-done(((f32[8,1,832,256]{3,2,1,0:T(8,128)}), f32[8,1,832,256]{3,2,1,0:T(8,128)}, u32[]{:S(2)}, u32[]{:S(2)}) %all-to-all-start.2) | async-done | bytes 6815776 | tf_op jit(solution)/shard_map/all_to_all | solution.py:179
  514.5 5.5 all-to-all-start.4
  520.0 6.7 mix_pieces.7
  530.7 3.1 collective-permute-done.5.refs_3_
  535.8 12.5 %finish.6 = (bf16[6656,1024]{1,0:T(8,128)(2,1)}, f32[26,8]{1,0:T(8,128)S(1)}) custom-call(f32[2,1664,256]{2,1,0:T(8,128)S(1)} %copy-done.12, f32[2,1664,256]{2,1,0:T(8,128)} %collective-permute-done.3.refs_1_, f32[2,1664,256]{2,1,0:T(8,128)} %collective-permute-done.4.refs_2_, ...), custom_call_target="tpu_custom_call", output_to_operand_aliasing={{0}: (4, {})} | custom-call | flops 999999995904 | bytes 4000000000 | tf_op jit(solution)/shard_map/finish/pallas_call | solution.py:472
  548.5 11.6 %make_pieces.9.refs_1_ = f32[8,1,208,256]{3,2,1,0:T(8,128)} custom-call(bf16[208,208]{1,0:T(8,128)(2,1)S(1)} %copy-done.6, bf16[256,256]{1,0:T(8,128)(2,1)S(1)} %copy-done.4, bf16[3328,2048]{1,0:T(8,128)(2,1)} %refs_1_.9, bf16[3328,2048]{1,0:T(8,128)(2,1)} %refs_1_.9, f32[2,13,8]{2,1,0:T(8,128)S(1)} %copy.25.refs_2_), custom_call_target="tpu_custom_call" | custom-call | tf_op jit(solution)/shard_map/make_pieces/pallas_call | solution.py:319
  560.1 35.0 %all-to-all-done.4.refs_0_ = f32[8,1,416,256]{3,2,1,0:T(8,128)} async-done(((f32[8,1,416,256]{3,2,1,0:T(8,128)}), f32[8,1,416,256]{3,2,1,0:T(8,128)}, u32[]{:S(2)}, u32[]{:S(2)}) %all-to-all-start.4) | async-done | bytes 3407904 | tf_op jit(solution)/shard_map/all_to_all | solution.py:179
  595.0 5.3 all-to-all-start.3
  600.3 3.7 mix_pieces.8
  607.4 6.1 finish.7
  613.8 25.2 %all-to-all-done.3.refs_0_ = f32[8,1,208,256]{3,2,1,0:T(8,128)} async-done(((f32[8,1,208,256]{3,2,1,0:T(8,128)}), f32[8,1,208,256]{3,2,1,0:T(8,128)}, u32[]{:S(2)}, u32[]{:S(2)}) %all-to-all-start.3) | async-done | bytes 1703968 | tf_op jit(solution)/shard_map/all_to_all | solution.py:179
  648.0 4.9 finish.8
  653.6 9.6 %collective-permute-done.11.refs_7_ = f32[2,208,256]{2,1,0:T(8,128)} collective-permute-done((f32[2,208,256]{2,1,0:T(8,128)}, f32[2,208,256]{2,1,0:T(8,128)}, u32[]{:S(2)}, u32[]{:S(2)}) %collective-permute-start.11) | collective-permute-done | bytes 426016 | tf_op jit(solution)/shard_map/ppermute | solution.py:198
  666.2 3.4 finish.9
  (100 shorter events, 39.9 us)
Async XLA Ops:
  14.0 48.0 %all-to-all-start = ((f32[8,1,208,256]{3,2,1,0:T(8,128)}), f32[8,1,208,256]{3,2,1,0:T(8,128)S(1)}, u32[]{:S(2)}, u32[]{:S(2)}) async-start(f32[8,1,208,256]{3,2,1,0:T(8,128)} %make_pieces.5.refs_2_), calls=%async_computation | async-start | bytes 3407872 | tf_op jit(solution)/shard_map/all_to_all | solution.py:179
  62.0 299.5 %all-to-all-start.1 = ((f32[8,1,1664,256]{3,2,1,0:T(8,128)}), f32[8,1,1664,256]{3,2,1,0:T(8,128)}, u32[]{:S(2)}, u32[]{:S(2)}) async-start(f32[8,1,1664,256]{3,2,1,0:T(8,128)} %make_pieces.6.refs_1_), calls=%async_computation.1 | async-start | bytes 27262976 | tf_op jit(solution)/shard_map/all_to_all | solution.py:179
  74.0 311.5 %collective-permute-start = (f32[2,208,256]{2,1,0:T(8,128)}, f32[2,208,256]{2,1,0:T(8,128)S(1)}, u32[]{:S(2)}, u32[]{:S(2)}) collective-permute-start(f32[2,208,256]{2,1,0:T(8,128)} %get-tuple-element.33), channel_id=1, source_target_pairs={{0,1},{1,0},{2,3},{3,2},{4,5},{5,4},{6,7},{7,6},{8,9},{9,8},{10,11... | collective-permute-start | bytes 1277960 | tf_op jit(solution)/shard_map/ppermute | solution.py:198
  75.5 310.5 %collective-permute-start.1 = (f32[2,208,256]{2,1,0:T(8,128)}, f32[2,208,256]{2,1,0:T(8,128)S(1)}, u32[]{:S(2)}, u32[]{:S(2)}) collective-permute-start(f32[2,208,256]{2,1,0:T(8,128)} %get-tuple-element.34), channel_id=1, source_target_pairs={{0,2},{1,3},{2,0},{3,1},{4,6},{5,7},{6,4},{7,5},{8,10},{9,11},{10,... | collective-permute-start | bytes 1277960 | tf_op jit(solution)/shard_map/ppermute | solution.py:198
  76.7 309.3 %collective-permute-start.2 = (f32[2,208,256]{2,1,0:T(8,128)}, f32[2,208,256]{2,1,0:T(8,128)S(1)}, u32[]{:S(2)}, u32[]{:S(2)}) collective-permute-start(f32[2,208,256]{2,1,0:T(8,128)} %get-tuple-element.35), channel_id=1, source_target_pairs={{0,3},{1,2},{2,1},{3,0},{4,7},{5,6},{6,5},{7,4},{8,11},{9,10},{10,... | collective-permute-start | bytes 1277960 | tf_op jit(solution)/shard_map/ppermute | solution.py:198
  361.5 153.0 %all-to-all-start.2 = ((f32[8,1,832,256]{3,2,1,0:T(8,128)}), f32[8,1,832,256]{3,2,1,0:T(8,128)}, u32[]{:S(2)}, u32[]{:S(2)}) async-start(f32[8,1,832,256]{3,2,1,0:T(8,128)} %make_pieces.7.refs_1_), calls=%async_computation.2 | async-start | bytes 13631488 | tf_op jit(solution)/shard_map/all_to_all | solution.py:179
  369.8 16.3 %copy-start.8 = (f32[2,208,256]{2,1,0:T(8,128)S(1)}, f32[2,208,256]{2,1,0:T(8,128)}, u32[]{:S(2)}) copy-start(f32[2,208,256]{2,1,0:T(8,128)} %copy-done.7) | copy-start | bytes 1277956
  382.4 147.9 %collective-permute-start.3 = (f32[2,1664,256]{2,1,0:T(8,128)}, f32[2,1664,256]{2,1,0:T(8,128)}, u32[]{:S(2)}, u32[]{:S(2)}) collective-permute-start(f32[2,1664,256]{2,1,0:T(8,128)} %get-tuple-element.37), channel_id=1, source_target_pairs={{0,1},{1,0},{2,3},{3,2},{4,5},{5,4},{6,7},{7,6},{8,9},{9,8},{10,11... | collective-permute-start | bytes 10223624 | tf_op jit(solution)/shard_map/ppermute | solution.py:198
  384.3 146.4 %collective-permute-start.4 = (f32[2,1664,256]{2,1,0:T(8,128)}, f32[2,1664,256]{2,1,0:T(8,128)}, u32[]{:S(2)}, u32[]{:S(2)}) collective-permute-start(f32[2,1664,256]{2,1,0:T(8,128)} %get-tuple-element.38), channel_id=1, source_target_pairs={{0,2},{1,3},{2,0},{3,1},{4,6},{5,7},{6,4},{7,5},{8,10},{9,11},{10,... | collective-permute-start | bytes 10223624 | tf_op jit(solution)/shard_map/ppermute | solution.py:198
  385.5 148.3 %collective-permute-start.5 = (f32[2,1664,256]{2,1,0:T(8,128)}, f32[2,1664,256]{2,1,0:T(8,128)}, u32[]{:S(2)}, u32[]{:S(2)}) collective-permute-start(f32[2,1664,256]{2,1,0:T(8,128)} %get-tuple-element.39), channel_id=1, source_target_pairs={{0,3},{1,2},{2,1},{3,0},{4,7},{5,6},{6,5},{7,4},{8,11},{9,10},{10,... | collective-permute-start | bytes 10223624 | tf_op jit(solution)/shard_map/ppermute | solution.py:198
  514.5 80.5 %all-to-all-start.4 = ((f32[8,1,416,256]{3,2,1,0:T(8,128)}), f32[8,1,416,256]{3,2,1,0:T(8,128)}, u32[]{:S(2)}, u32[]{:S(2)}) async-start(f32[8,1,416,256]{3,2,1,0:T(8,128)} %make_pieces.8.refs_1_), calls=%async_computation.4 | async-start | bytes 6815744 | tf_op jit(solution)/shard_map/all_to_all | solution.py:179
  526.7 80.2 %collective-permute-start.6 = (f32[2,832,256]{2,1,0:T(8,128)}, f32[2,832,256]{2,1,0:T(8,128)}, u32[]{:S(2)}, u32[]{:S(2)}) collective-permute-start(f32[2,832,256]{2,1,0:T(8,128)} %get-tuple-element.44), channel_id=1, source_target_pairs={{0,1},{1,0},{2,3},{3,2},{4,5},{5,4},{6,7},{7,6},{8,9},{9,8},{10,11... | collective-permute-start | bytes 5111816 | tf_op jit(solution)/shard_map/ppermute | solution.py:198
  528.4 79.0 %collective-permute-start.7 = (f32[2,832,256]{2,1,0:T(8,128)}, f32[2,832,256]{2,1,0:T(8,128)}, u32[]{:S(2)}, u32[]{:S(2)}) collective-permute-start(f32[2,832,256]{2,1,0:T(8,128)} %get-tuple-element.45), channel_id=1, source_target_pairs={{0,2},{1,3},{2,0},{3,1},{4,6},{5,7},{6,4},{7,5},{8,10},{9,11},{10,... | collective-permute-start | bytes 5111816 | tf_op jit(solution)/shard_map/ppermute | solution.py:198
  530.3 77.1 %collective-permute-start.8 = (f32[2,832,256]{2,1,0:T(8,128)}, f32[2,832,256]{2,1,0:T(8,128)}, u32[]{:S(2)}, u32[]{:S(2)}) collective-permute-start(f32[2,832,256]{2,1,0:T(8,128)} %get-tuple-element.46), channel_id=1, source_target_pairs={{0,3},{1,2},{2,1},{3,0},{4,7},{5,6},{6,5},{7,4},{8,11},{9,10},{10,... | collective-permute-start | bytes 5111816 | tf_op jit(solution)/shard_map/ppermute | solution.py:198
  595.0 44.0 %all-to-all-start.3 = ((f32[8,1,208,256]{3,2,1,0:T(8,128)}), f32[8,1,208,256]{3,2,1,0:T(8,128)}, u32[]{:S(2)}, u32[]{:S(2)}) async-start(f32[8,1,208,256]{3,2,1,0:T(8,128)} %make_pieces.9.refs_1_), calls=%async_computation.3 | async-start | bytes 3407872 | tf_op jit(solution)/shard_map/all_to_all | solution.py:179
  604.0 41.9 %collective-permute-start.12 = (f32[2,416,256]{2,1,0:T(8,128)}, f32[2,416,256]{2,1,0:T(8,128)}, u32[]{:S(2)}, u32[]{:S(2)}) collective-permute-start(f32[2,416,256]{2,1,0:T(8,128)} %get-tuple-element.54), channel_id=1, source_target_pairs={{0,1},{1,0},{2,3},{3,2},{4,5},{5,4},{6,7},{7,6},{8,9},{9,8},{10,11... | collective-permute-start | bytes 2555912 | tf_op jit(solution)/shard_map/ppermute | solution.py:198
  605.7 40.3 %collective-permute-start.13 = (f32[2,416,256]{2,1,0:T(8,128)}, f32[2,416,256]{2,1,0:T(8,128)}, u32[]{:S(2)}, u32[]{:S(2)}) collective-permute-start(f32[2,416,256]{2,1,0:T(8,128)} %get-tuple-element.55), channel_id=1, source_target_pairs={{0,2},{1,3},{2,0},{3,1},{4,6},{5,7},{6,4},{7,5},{8,10},{9,11},{10,... | collective-permute-start | bytes 2555912 | tf_op jit(solution)/shard_map/ppermute | solution.py:198
  606.9 39.0 %collective-permute-start.14 = (f32[2,416,256]{2,1,0:T(8,128)}, f32[2,416,256]{2,1,0:T(8,128)}, u32[]{:S(2)}, u32[]{:S(2)}) collective-permute-start(f32[2,416,256]{2,1,0:T(8,128)} %get-tuple-element.56), channel_id=1, source_target_pairs={{0,3},{1,2},{2,1},{3,0},{4,7},{5,6},{6,5},{7,4},{8,11},{9,10},{10,... | collective-permute-start | bytes 2555912 | tf_op jit(solution)/shard_map/ppermute | solution.py:198
  607.4 38.6 %copy-start.9 = (f32[2,208,256]{2,1,0:T(8,128)S(1)}, f32[2,208,256]{2,1,0:T(8,128)}, u32[]{:S(2)}) copy-start(f32[2,208,256]{2,1,0:T(8,128)} %copy-done.7) | copy-start | bytes 1277956
  607.4 38.6 %copy-start.14 = (f32[2,208,256]{2,1,0:T(8,128)S(1)}, f32[2,208,256]{2,1,0:T(8,128)}, u32[]{:S(2)}) copy-start(f32[2,208,256]{2,1,0:T(8,128)} %copy-done.13) | copy-start | bytes 1277956
  613.7 39.2 %copy-start.25 = (f32[2,6,8]{1,0,2:T(2,128)}, f32[2,6,8]{1,0,2:T(2,128)S(1)}, u32[]{:S(2)}) copy-start(f32[2,6,8]{1,0,2:T(2,128)S(1)} %reshape.24) | copy-start | bytes 1156
  642.1 11.5 %collective-permute-start.10 = (f32[2,208,256]{2,1,0:T(8,128)}, f32[2,208,256]{2,1,0:T(8,128)}, u32[]{:S(2)}, u32[]{:S(2)}) collective-permute-start(f32[2,208,256]{2,1,0:T(8,128)} %get-tuple-element.52), channel_id=1, source_target_pairs={{0,2},{1,3},{2,0},{3,1},{4,6},{5,7},{6,4},{7,5},{8,10},{9,11},{10,... | collective-permute-start | bytes 1277960 | tf_op jit(solution)/shard_map/ppermute | solution.py:198
  643.3 19.9 %collective-permute-start.11 = (f32[2,208,256]{2,1,0:T(8,128)}, f32[2,208,256]{2,1,0:T(8,128)}, u32[]{:S(2)}, u32[]{:S(2)}) collective-permute-start(f32[2,208,256]{2,1,0:T(8,128)} %get-tuple-element.53), channel_id=1, source_target_pairs={{0,3},{1,2},{2,1},{3,0},{4,7},{5,6},{6,5},{7,4},{8,11},{9,10},{10,... | collective-permute-start | bytes 1277960 | tf_op jit(solution)/shard_map/ppermute | solution.py:198
  646.0 17.3 %collective-permute-start.9 = (f32[2,208,256]{2,1,0:T(8,128)}, f32[2,208,256]{2,1,0:T(8,128)}, u32[]{:S(2)}, u32[]{:S(2)}) collective-permute-start(f32[2,208,256]{2,1,0:T(8,128)} %get-tuple-element.51), channel_id=1, source_target_pairs={{0,1},{1,0},{2,3},{3,2},{4,5},{5,4},{6,7},{7,6},{8,9},{9,8},{10,11... | collective-permute-start | bytes 1277960 | tf_op jit(solution)/shard_map/ppermute | solution.py:198
  (25 other events, 97.3 us)
